TPU v7x, 32 devices: a whole 2x2x4 slice. The times are simulated.
32 devices in a mesh: enc: 4 (over z), mb: 2 (over core), tp: 4 (over y, x).
Axes of the slice: x: 2, y: 2, z: 4, core: 2. Of those that a mesh axis runs over, the one named last changes fastest.
Arguments:
- patches: bfloat16 [4, 2, 256, 1280], P('enc', 'mb', 'tp'), may hold values from -6 to 6
- patch_counts: int32 [4, 2, 8], P('enc', 'mb'), may hold values from 4 to 32, as said below
- dest_pos: int32 [4, 2, 64], P('enc', 'mb'), may hold values from 0 to 511, as said below
- merge_gain: float32 [1280], replicated, may hold values from 0.25 to 1.75
- merge_bias: float32 [1280], replicated, may hold values from -3 to 3
- up_weight: bfloat16 [5120, 5120], P(('enc', 'mb'), 'tp'), may hold values from -0.078125 to 0.078125
- up_bias: float32 [5120], replicated, may hold values from -3 to 3
- down_weight: bfloat16 [5120, 8192], P('tp', ('enc', 'mb')), may hold values from -0.078125 to 0.078125
- down_bias: float32 [8192], replicated, may hold values from -3 to 3
- text_embed: bfloat16 [4, 2, 512, 8192], P('enc', 'mb', 'tp'), may hold values from -6 to 6
- norm_gain: float32 [8192], replicated, may hold values from 0.25 to 1.75
- kv_weight: bfloat16 [8192, 2048], P('tp'), may hold values from -0.0625 to 0.0625
- kv_bias: float32 [2048], replicated, may hold values from -3 to 3
Outputs:
- embedded: bfloat16 [4, 2, 512, 8192], P('enc', 'mb', 'tp')
- keys_values: bfloat16 [4, 2, 512, 2048], P('enc', 'mb', 'tp')
Inputs may be any that keep to these rules, and one draw needn't show every extreme that they name: `patch_counts`: each image's patch count is four times its merged rows; in every sequence some image has 32 patches. The image slots of enc index e and mb index m feed sequence (e, m); slot j of device t of tp is image t * 2 + j. `dest_pos`: the 8 slots of an image hold consecutive positions; slots past the image's merged rows are not live and their positions are used by no live slot; no two live slots of a sequence share a position.
All inputs are finite; a program needn't handle non-finite values.
Results may differ from a plain program's by a relative error of at most 0.02.
Values may be sent and summed in bfloat16 or wider, within the bound.
A program may use at most 128 MiB of HBM per device.

v0:
```python
import jax
import jax.numpy as jnp
from jax import lax
from jax.sharding import PartitionSpec as P

SLOT = 8


def layer_norm(rows, gain, bias):
    values = rows.astype(jnp.float32)
    center = values - jnp.mean(values, axis=-1, keepdims=True)
    spread = jnp.mean(center * center, axis=-1, keepdims=True)
    return center * lax.rsqrt(spread + 1e-06) * gain + bias


def root_scale(values, gain):
    return (
        values * lax.rsqrt(jnp.mean(values * values, axis=-1, keepdims=True) + 1e-06) * gain
    ).astype(jnp.bfloat16)


def per_device(
    patches,
    patch_counts,
    dest_pos,
    merge_gain,
    merge_bias,
    up_weight,
    up_bias,
    down_weight,
    down_bias,
    text_embed,
    norm_gain,
    kv_weight,
    kv_bias,
):
    text = text_embed[0, 0]
    tokens = text.shape[0]
    normal = layer_norm(patches[0, 0], merge_gain, merge_bias).astype(jnp.bfloat16)
    merged = normal.reshape(normal.shape[0] // 4, normal.shape[1] * 4)
    group_rows = lax.all_gather(merged, "tp", axis=0, tiled=True)
    raised = jnp.dot(
        group_rows,
        lax.all_gather(up_weight, ("enc", "mb"), axis=0, tiled=True),
        preferred_element_type=jnp.float32,
    )
    unit_start = lax.axis_index("tp") * up_weight.shape[1]
    own_bias = lax.dynamic_slice_in_dim(up_bias, unit_start, up_weight.shape[1], 0)
    hidden = jax.nn.gelu(raised + own_bias, approximate=False).astype(jnp.bfloat16)
    down_full = lax.all_gather(down_weight, ("enc", "mb"), axis=1, tiled=True)
    rows = hidden
    own = lax.psum_scatter(
        jnp.dot(rows, down_full, preferred_element_type=jnp.float32).astype(jnp.bfloat16),
        "tp",
        scatter_dimension=0,
        tiled=True,
    ).astype(jnp.float32)
    visual = (own + down_bias).astype(jnp.bfloat16)
    visual_all = lax.all_gather(visual, "tp", axis=0, tiled=True)
    live_rows = patch_counts[0, 0] // 4
    live = (jnp.arange(SLOT, dtype=jnp.int32)[None, :] < live_rows[:, None]).reshape(-1)
    first = lax.axis_index("tp") * tokens
    places = first + jnp.arange(tokens, dtype=jnp.int32)
    select = (dest_pos[0, 0][None, :] == places[:, None]) & live[None, :]
    picked = jnp.dot(select.astype(jnp.bfloat16), visual_all, preferred_element_type=jnp.float32)
    present = jnp.any(select, axis=1)
    restored = picked.astype(jnp.bfloat16)
    embedded = jnp.where(present[:, None], restored, text)
    normed = root_scale(embedded.astype(jnp.float32), norm_gain)
    feature_rows = lax.all_to_all(normed, "tp", split_axis=1, concat_axis=0, tiled=True)
    rows = feature_rows
    kv_total = lax.psum_scatter(
        jnp.dot(rows, kv_weight, preferred_element_type=jnp.float32).astype(jnp.bfloat16),
        "tp",
        scatter_dimension=0,
        tiled=True,
    ).astype(jnp.float32)
    keys_values = (kv_total + kv_bias).astype(jnp.bfloat16)
    return (embedded[None, None], keys_values[None, None])


def solution(mesh):
    return jax.shard_map(
        per_device,
        mesh=mesh,
        in_specs=(
            P("enc", "mb", "tp", None),
            P("enc", "mb", None),
            P("enc", "mb", None),
            P(),
            P(),
            P(("enc", "mb"), "tp"),
            P(),
            P("tp", ("enc", "mb")),
            P(),
            P("enc", "mb", "tp", None),
            P(),
            P("tp", None),
            P(),
        ),
        out_specs=(P("enc", "mb", "tp", None), P("enc", "mb", "tp", None)),
        check_vma=False,
    )
```

profile of v0, /device:TPU:0, one launch (start us, length us, event | category | flops | bytes accessed | tf_op | source)
XLA Modules:
  0.0 466.8 jit_solution(17538607243724765793)
XLA Ops:
  7.2 0.7 all-gather.4.cloned.1.call-update
  8.0 0.7 all-gather.6.cloned.1.call-update
  8.7 0.1 reshape.103
  8.8 0.1 convert_reduce_fusion
  9.0 0.1 div.31
  9.1 0.2 fusion.9
  9.3 0.1 rsqrt.20
  9.4 0.1 mul.69
  9.5 0.1 copy.19
  9.6 0.1 sub.20
  9.7 0.1 copy.18
  9.9 0.8 dynamic_slice.3
  10.6 0.1 add_convert_fusion.2
  10.7 12.0 %all_gather.12 = bf16[64,5120]{1,0:T(8,128)(2,1)S(1)} all-gather(bf16[16,5120]{1,0:T(8,128)(2,1)S(1)} %add_convert_fusion.2), channel_id=1, replica_groups=mesh['enc'=4,'mb'=2,'tp'=4] {'tp'}, dimensions={0}, use_global_device_ids=true | all-gather | bytes 819200 | tf_op jit(solution)/shard_map/all_gather | solution.py:41
  22.8 110.7 %all-gather.4.cloned.1.call-done = bf16[5120,1280]{1,0:T(8,128)(2,1)} async-done(((bf16[640,1280]{1,0:T(8,128)(2,1)}), bf16[5120,1280]{1,0:T(8,128)(2,1)}) %all-gather.4.cloned.1.call-update) | async-done | bytes 13107216 | tf_op jit(solution)/shard_map/all_gather | solution.py:44
  133.4 7.7 %fusion.7 = bf16[64,1280]{1,0:T(8,128)(2,1)S(1)} fusion(bf16[64,5120]{1,0:T(8,128)(2,1)S(1)} %all_gather.12, bf16[5120,1280]{1,0:T(8,128)(2,1)} %all-gather.4.cloned.1.call-done, f32[1280]{0:T(1024)S(1)} %dynamic_slice.3), kind=kOutput, calls=%fused_computation.17 | convolution fusion | flops 844267520 | bytes 13931520 | tf_op jit(solution)/shard_map/dot_general | solution.py:42
  141.1 177.6 %all-gather.6.cloned.1.call-done = bf16[1280,8192]{1,0:T(8,128)(2,1)} async-done(((bf16[1280,1024]{1,0:T(8,128)(2,1)}), bf16[1280,8192]{1,0:T(8,128)(2,1)}) %all-gather.6.cloned.1.call-update) | async-done | bytes 20971536 | tf_op jit(solution)/shard_map/all_gather | solution.py:50
  318.8 11.8 %convolution_convert_fusion.1 = bf16[64,8192]{1,0:T(8,128)(2,1)} fusion(bf16[64,1280]{1,0:T(8,128)(2,1)S(1)} %fusion.7, bf16[1280,8192]{1,0:T(8,128)(2,1)} %all-gather.6.cloned.1.call-done), kind=kOutput, calls=%fused_computation.2 | convolution fusion | flops 1342701568 | bytes 22183936 | tf_op jit(solution)/shard_map/dot_general | solution.py:53
  330.6 26.0 %reduce-scatter.3.cloned.1.call-done = bf16[16,8192]{1,0:T(8,128)(2,1)} async-done(((bf16[64,8192]{1,0:T(8,128)(2,1)}), bf16[16,8192]{1,0:T(8,128)(2,1)}) %reduce-scatter.3.cloned.1.call-update) | async-done | bytes 262160 | tf_op jit(solution)/shard_map/reduce_scatter | solution.py:52
  356.6 1.7 add_convert_fusion.1
  358.4 0.1 iota_compare_fusion
  358.5 0.1 lt.26
  358.6 0.1 fusion.17
  358.7 27.0 %all-gather.8.cloned.1.call-done = bf16[64,8192]{1,0:T(8,128)(2,1)} async-done(((bf16[16,8192]{1,0:T(8,128)(2,1)}), bf16[64,8192]{1,0:T(8,128)(2,1)}) %all-gather.8.cloned.1.call-update) | async-done | bytes 1048592 | tf_op jit(solution)/shard_map/all_gather | solution.py:59
  385.7 2.5 fusion.1
  388.2 0.6 fusion.3
  388.8 0.2 copy.21
  389.1 0.4 copy-done
  389.5 28.2 %all_to_all.19 = bf16[128,4,2048]{2,0,1:T(8,128)(2,1)S(1)} all-to-all(bf16[128,4,2048]{2,0,1:T(8,128)(2,1)S(1)} %bitcast.41), channel_id=1, replica_groups=mesh['enc'=4,'mb'=2,'tp'=4] {'tp'}, dimensions={1} | all-to-all | bytes 4194304 | tf_op jit(solution)/shard_map/all_to_all | solution.py:70
  417.8 5.8 %convolution_convert_fusion.2 = bf16[512,2048]{1,0:T(8,128)(2,1)} fusion(bf16[512,2048]{1,0:T(8,128)(2,1)S(1)} %bitcast.43, bf16[2048,2048]{1,0:T(8,128)(2,1)S(1)} %bitcast.51), kind=kOutput, calls=%fused_computation.8 | convolution fusion | flops 4296015872 | bytes 12582912 | tf_op jit(solution)/shard_map/dot_general | solution.py:73
  423.6 34.8 %reduce-scatter.5.cloned.1.call-done = bf16[128,2048]{1,0:T(8,128)(2,1)} async-done(((bf16[512,2048]{1,0:T(8,128)(2,1)}), bf16[128,2048]{1,0:T(8,128)(2,1)}) %reduce-scatter.5.cloned.1.call-update) | async-done | bytes 524304 | tf_op jit(solution)/shard_map/reduce_scatter | solution.py:72
  458.4 1.9 fusion.4
  (41 shorter events, 0.4 us)
Async XLA Ops:
  7.2 1.6 copy-start.1
  7.2 2.6 copy-start.5
  7.2 2.6 copy-start.6
  7.2 126.2 %all-gather.4.cloned.1.call-start = ((), (), s32[]{:S(2)}) async-start(), calls=%async_computation.3 | async-start | bytes 14745600 | tf_op jit(solution)/shard_map/all_gather | solution.py:44
  7.9 310.9 %all-gather.6.cloned.1.call-start = ((), (), s32[]{:S(2)}) async-start(), calls=%async_computation.4 | async-start | bytes 23592960 | tf_op jit(solution)/shard_map/all_gather | solution.py:50
  8.7 348.0 %reduce-scatter.3.cloned.1.call-start = ((), (), s32[]{:S(2)}) async-start(), calls=%async_computation.5 | async-start | bytes 1310720 | tf_op jit(solution)/shard_map/reduce_scatter | solution.py:52
  141.1 215.5 %copy-start.3 = (f32[8192]{0:T(1024)S(1)}, f32[8192]{0:T(1024)}, u32[]{:S(2)}) copy-start(f32[8192]{0:T(1024)} %param.21) | copy-start | bytes 98308
  141.1 217.3 %copy-start.9 = (s32[1,1,8]{2,1,0:T(1,128)S(1)}, s32[1,1,8]{2,1,0:T(1,128)}, u32[]{:S(2)}) copy-start(s32[1,1,8]{2,1,0:T(1,128)} %param.14) | copy-start | bytes 100
  141.1 217.5 %copy-start.7 = (s32[1,1,64]{2,1,0:T(1,128)S(1)}, s32[1,1,64]{2,1,0:T(1,128)}, u32[]{:S(2)}) copy-start(s32[1,1,64]{2,1,0:T(1,128)} %param.15) | copy-start | bytes 772
  141.1 244.6 %copy-start.8 = (bf16[1,1,128,8192]{3,2,1,0:T(8,128)(2,1)S(1)}, bf16[1,1,128,8192]{3,2,1,0:T(8,128)(2,1)}, u32[]{:S(2)}) copy-start(bf16[1,1,128,8192]{3,2,1,0:T(8,128)(2,1)} %param.22) | copy-start | bytes 6291460
  330.5 57.7 %copy-start.2 = (f32[8192]{0:T(1024)S(1)}, f32[8192]{0:T(1024)}, u32[]{:S(2)}) copy-start(f32[8192]{0:T(1024)} %param.23) | copy-start | bytes 98308
  330.6 55.2 %all-gather.8.cloned.1.call-start = ((), (), s32[]{:S(2)}) async-start(), calls=%async_computation.6 | async-start | bytes 1310720 | tf_op jit(solution)/shard_map/all_gather | solution.py:59
  358.4 100.0 %reduce-scatter.5.cloned.1.call-start = ((), (), s32[]{:S(2)}) async-start(), calls=%async_computation.7 | async-start | bytes 2621440 | tf_op jit(solution)/shard_map/reduce_scatter | solution.py:72
  385.7 32.0 %slice-start = ((s8[8388608]{0:T(1024)(128)(4,1)}), s8[4194304]{0:T(1024)(128)(4,1)S(1)}, s32[]{:S(2)}) async-start(s8[8388608]{0:T(1024)(128)(4,1)} %bitcast.50), calls=%async_computation.8 | async-start | bytes 8388608
  388.2 1.3 copy-start
  388.2 29.5 %slice-start.1 = ((s8[8388608]{0:T(1024)(128)(4,1)}), s8[4194304]{0:T(1024)(128)(4,1)S(1)}, s32[]{:S(2)}) async-start(s8[8388608]{0:T(1024)(128)(4,1)} %bitcast.50), calls=%async_computation.9 | async-start | bytes 8388608
  417.8 40.6 %copy-start.4 = (f32[2048]{0:T(1024)S(1)}, f32[2048]{0:T(1024)}, u32[]{:S(2)}) copy-start(f32[2048]{0:T(1024)} %param.25) | copy-start | bytes 24580
Sparse Core Ops, SparseCore 0:
  9.7 123.7 all-gather.3
  135.0 183.7 all-gather.5
  330.7 25.8 reduce-scatter.2
  359.1 26.6 all-gather.7
  423.7 34.6 reduce-scatter.4
where the time goes:
time: 467 us
  waiting for transfers between devices  378 us (81%)
  blocking collectives  40.3 us (9%)
  matrix products  27.6 us (6%)
  between operations  14 us (3%)
  other arithmetic  4.85 us (1%)
    all_gather x1, waiting for transfers between devices, per_device(): down_full = lax.all_gather(down_weight, ('enc', 'mb'), axis=1, tiled=True)  178 us
    all_gather x1, waiting for transfers between devices, per_device(): lax.all_gather(up_weight, ('enc', 'mb'), axis=0, tiled=True)  111 us
    reduce_scatter x1, waiting for transfers between devices, per_device(): lax.psum_scatter(jnp.dot(rows, kv_weight, preferred_element_type=jnp.floa...  34.8 us
    all_to_all x1, blocking collectives, per_device(): lax.all_to_all(normed, 'tp', split_axis=1, concat_axis=0, tiled=True)  28.2 us
    all_gather x1, waiting for transfers between devices, per_device(): visual_all = lax.all_gather(visual, 'tp', axis=0, tiled=True)  27 us
    reduce_scatter x1, waiting for transfers between devices, per_device(): lax.psum_scatter(jnp.dot(rows, down_full, preferred_element_type=jnp.floa...  26 us
    all_gather x1, blocking collectives, per_device(): group_rows = lax.all_gather(merged, 'tp', axis=0, tiled=True)  12 us
    dot_general x1, matrix products, per_device(): jnp.dot(rows, down_full, preferred_element_type=jnp.float32)  11.8 us
  transfers between devices with their start and end apart: 5, of which 5 were waited for; matrix products, arithmetic and copies ran while one was open for 2% of the time, Pallas kernels for 0%

commit v1 on v0

v1 whole, which is shorter than its diff:
```python
import jax
import jax.numpy as jnp
from jax import lax
from jax.sharding import PartitionSpec as P

SLOT = 8
GROUP = ("enc", "mb")


def layer_norm(rows, gain, bias):
    values = rows.astype(jnp.float32)
    center = values - jnp.mean(values, axis=-1, keepdims=True)
    spread = jnp.mean(center * center, axis=-1, keepdims=True)
    return center * lax.rsqrt(spread + 1e-06) * gain + bias


def per_device(
    patches,
    patch_counts,
    dest_pos,
    merge_gain,
    merge_bias,
    up_weight,
    up_bias,
    down_weight,
    down_bias,
    text_embed,
    norm_gain,
    kv_weight,
    kv_bias,
):
    groups = lax.axis_size("enc") * lax.axis_size("mb")
    parts = lax.axis_size("tp")
    tp = lax.axis_index("tp")
    group = lax.axis_index("enc") * lax.axis_size("mb") + lax.axis_index("mb")
    text = text_embed[0, 0]
    tokens, width = text.shape
    feats = kv_weight.shape[0]
    units = up_weight.shape[1]
    cols = down_weight.shape[1]
    own_gain = lax.dynamic_slice_in_dim(norm_gain, tp * feats, feats, 0)

    text_cols = lax.all_to_all(text, "tp", split_axis=1, concat_axis=0, tiled=True)
    scaled = (text_cols.astype(jnp.float32) * own_gain).astype(jnp.bfloat16)
    text_part = jnp.dot(scaled, kv_weight, preferred_element_type=jnp.float32).astype(jnp.bfloat16)
    text_kv = lax.psum_scatter(text_part, "tp", scatter_dimension=0, tiled=True)

    normal = layer_norm(patches[0, 0], merge_gain, merge_bias).astype(jnp.bfloat16)
    own = normal.shape[0] // 4
    merged = normal.reshape(own, normal.shape[1] * 4)
    slices = lax.all_to_all(merged, GROUP, split_axis=1, concat_axis=0, tiled=True)
    rows = lax.all_gather(slices, "tp", axis=0, tiled=True)
    raised = jnp.dot(rows, up_weight, preferred_element_type=jnp.float32).astype(jnp.bfloat16)
    raised = raised.reshape(parts, groups, own, units).transpose(1, 0, 2, 3).reshape(-1, units)
    raised = lax.psum_scatter(raised, GROUP, scatter_dimension=0, tiled=True).astype(jnp.float32)
    own_bias = lax.dynamic_slice_in_dim(up_bias, tp * units, units, 0)
    hidden = jax.nn.gelu(raised + own_bias, approximate=False).astype(jnp.bfloat16)
    all_hidden = lax.all_gather(hidden, GROUP, axis=0, tiled=True)
    lowered = jnp.dot(all_hidden, down_weight, preferred_element_type=jnp.float32).astype(jnp.bfloat16)
    lowered = lowered.reshape(groups, parts, own, cols).transpose(1, 0, 2, 3).reshape(-1, cols)
    lowered = lax.psum_scatter(lowered, "tp", scatter_dimension=0, tiled=True).astype(jnp.float32)
    down_own = lax.dynamic_slice_in_dim(down_bias, group * cols, cols, 0)
    visual = (lowered + down_own).astype(jnp.bfloat16)
    visual = lax.all_to_all(visual, GROUP, split_axis=0, concat_axis=1, tiled=True)
    visual_all = lax.all_gather(visual, "tp", axis=0, tiled=True)

    visual_cols = lax.dynamic_slice_in_dim(visual_all, tp * feats, feats, 1)
    visual_scaled = (visual_cols.astype(jnp.float32) * own_gain).astype(jnp.bfloat16)
    visual_part = jnp.dot(visual_scaled, kv_weight, preferred_element_type=jnp.float32).astype(jnp.bfloat16)
    visual_kv = lax.psum(visual_part, "tp")

    live_rows = patch_counts[0, 0] // 4
    live = (jnp.arange(SLOT, dtype=jnp.int32)[None, :] < live_rows[:, None]).reshape(-1)
    places = tp * tokens + jnp.arange(tokens, dtype=jnp.int32)
    select = (dest_pos[0, 0][None, :] == places[:, None]) & live[None, :]
    picks = select.astype(jnp.bfloat16)
    present = jnp.any(select, axis=1)[:, None]
    picked = jnp.dot(picks, visual_all, preferred_element_type=jnp.float32).astype(jnp.bfloat16)
    embedded = jnp.where(present, picked, text)
    values = embedded.astype(jnp.float32)
    scale = lax.rsqrt(jnp.mean(values * values, axis=-1, keepdims=True) + 1e-06)
    picked_kv = jnp.dot(picks, visual_kv, preferred_element_type=jnp.float32)
    kv_total = jnp.where(present, picked_kv, text_kv.astype(jnp.float32)) * scale
    keys_values = (kv_total + kv_bias).astype(jnp.bfloat16)
    return (embedded[None, None], keys_values[None, None])


def solution(mesh):
    return jax.shard_map(
        per_device,
        mesh=mesh,
        in_specs=(
            P("enc", "mb", "tp", None),
            P("enc", "mb", None),
            P("enc", "mb", None),
            P(),
            P(),
            P(("enc", "mb"), "tp"),
            P(),
            P("tp", ("enc", "mb")),
            P(),
            P("enc", "mb", "tp", None),
            P(),
            P("tp", None),
            P(),
        ),
        out_specs=(P("enc", "mb", "tp", None), P("enc", "mb", "tp", None)),
        check_vma=False,
    )
```

time: 467 us -> 279 us (0.60)
  waiting for transfers between devices: 378 us -> 172 us
  blocking collectives: 40.3 us -> 23.9 us
  local copies, waits for them, and re-layouts: 2.29 us -> 18.2 us
  starting transfers between devices: 0.2 us -> 9.17 us
  other arithmetic: 4.85 us -> 13.1 us
    all_gather x2 -> x1, waiting for transfers between devices: 288 us -> 21.6 us  [per_device(): all_hidden = lax.all_gather(hidden, GROUP, axis=0, tiled=True)]
    psum x0 -> x1, waiting for transfers between devices: none -> 46.3 us  [per_device(): visual_kv = lax.psum(visual_part, 'tp')]
    reduce_scatter x2 -> x3, waiting for transfers between devices: 60.8 us -> 90 us  [the longest x1 31 us: per_device(): lax.psum_scatter(raised, GROUP, scatter_dimension=0, tiled=True)]
    all_to_all x1, blocking collectives: 28.2 us -> 13.3 us  [per_device(): lax.all_to_all(merged, GROUP, split_axis=1, concat_axis=0, tiled=True)]
    all_gather x1, waiting for transfers between devices: 27 us -> 13.9 us  [per_device(): visual_all = lax.all_gather(visual, 'tp', axis=0, tiled=True)]
    all_to_all x0 -> x2, starting transfers between devices: none -> 8.93 us  [the longest x1 4.47 us: per_device(): lax.all_to_all(visual, GROUP, split_axis=0, concat_axis=1, tiled=True)]
    convert_element_type x2 -> x4, other arithmetic: 2.28 us -> 10.5 us  [the longest x2 6.48 us: per_device(): scaled = (text_cols.astype(jnp.float32) * own_gain).astype(jnp.bfloat16)]
    convert_element_type x0 -> x2, local copies, waits for them, and re-layouts: none -> 5.44 us  [the longest x1 5.42 us: per_device(): scaled = (text_cols.astype(jnp.float32) * own_gain).astype(jnp.bfloat16)]
  transfers between devices with their start and end apart: 5 -> 8, of which waited for: 5 -> 7; matrix products, arithmetic and copies ran while one was open for 2% -> 14% of each run, Pallas kernels for 0% -> 0%
where the time goes in v1:
time: 279 us; the launch traced here: 278 us
  waiting for transfers between devices  172 us (62%)
  matrix products  26.9 us (10%)
  blocking collectives  23.9 us (9%)
  local copies, waits for them, and re-layouts  18.2 us (7%)
  between operations  14.3 us (5%)
  other arithmetic  13.1 us (5%)
  starting transfers between devices  9.17 us (3%)
    psum x1, waiting for transfers between devices, per_device(): visual_kv = lax.psum(visual_part, 'tp')  46.3 us
    reduce_scatter x1, waiting for transfers between devices, per_device(): lax.psum_scatter(raised, GROUP, scatter_dimension=0, tiled=True)  31 us
    reduce_scatter x1, waiting for transfers between devices, per_device(): lax.psum_scatter(lowered, 'tp', scatter_dimension=0, tiled=True)  30.7 us
    reduce_scatter x1, waiting for transfers between devices, per_device(): text_kv = lax.psum_scatter(text_part, 'tp', scatter_dimension=0, tiled=True)  28.3 us
    all_gather x1, waiting for transfers between devices, per_device(): all_hidden = lax.all_gather(hidden, GROUP, axis=0, tiled=True)  21.6 us
    all_gather x1, waiting for transfers between devices, per_device(): visual_all = lax.all_gather(visual, 'tp', axis=0, tiled=True)  13.9 us
    all_to_all x1, blocking collectives, per_device(): lax.all_to_all(merged, GROUP, split_axis=1, concat_axis=0, tiled=True)  13.3 us
    all_gather x1, blocking collectives, per_device(): rows = lax.all_gather(slices, 'tp', axis=0, tiled=True)  10.6 us
  transfers between devices with their start and end apart: 8, of which 7 were waited for; matrix products, arithmetic and copies ran while one was open for 14% of the time, Pallas kernels for 0%

profile of v1, /device:TPU:0, one launch (start us, length us, event | category | flops | bytes accessed | tf_op | source)
XLA Modules:
  0.0 278.1 jit_solution(8319657013633487927)
XLA Ops:
  7.2 1.2 convert_reduce_fusion
  8.4 1.1 fusion.10
  9.6 1.0 reshape.147
  10.6 0.7 mul.97
  11.3 0.7 add.103
  12.7 13.3 %all_to_all.48 = bf16[16,8,640]{2,0,1:T(8,128)(2,1)S(1)} all-to-all(bf16[16,8,640]{2,0,1:T(8,128)(2,1)S(1)} %copy.48), channel_id=1, replica_groups=mesh['enc'=4,'mb'=2,'tp'=4] {'enc','mb'}, dimensions={1} | all-to-all | bytes 327680 | tf_op jit(solution)/shard_map/all_to_all | solution.py:51
  26.1 10.6 %all_gather.9 = bf16[512,640]{1,0:T(8,128)(2,1)S(1)} all-gather(bf16[128,640]{1,0:T(8,128)(2,1)S(1)} %bitcast.62), channel_id=1, replica_groups=mesh['enc'=4,'mb'=2,'tp'=4] {'tp'}, dimensions={0}, use_global_device_ids=true | all-gather | bytes 819200 | tf_op jit(solution)/shard_map/all_gather | solution.py:52
  36.6 2.6 convolution_convert_fusion.1
  39.2 1.2 copy.49
  40.5 0.8 dynamic_slice.12
  41.3 31.0 %reduce-scatter.4.cloned.1.call-done = bf16[64,1280]{1,0:T(8,128)(2,1)} async-done(((bf16[512,1280]{1,0:T(8,128)(2,1)}), bf16[64,1280]{1,0:T(8,128)(2,1)}) %reduce-scatter.4.cloned.1.call-update) | async-done | bytes 163856 | tf_op jit(solution)/shard_map/reduce_scatter | solution.py:55
  72.3 2.3 fusion.8
  74.7 21.6 %all-gather.3.cloned.1.call-done = bf16[512,1280]{1,0:T(8,128)(2,1)} async-done(((bf16[64,1280]{1,0:T(8,128)(2,1)}), bf16[512,1280]{1,0:T(8,128)(2,1)}) %all-gather.3.cloned.1.call-update) | async-done | bytes 1310736 | tf_op jit(solution)/shard_map/all_gather | solution.py:58
  96.3 2.8 %convolution_convert_fusion.4 = bf16[512,1024]{1,0:T(8,128)(2,1)S(1)} fusion(bf16[512,1280]{1,0:T(8,128)(2,1)} %all-gather.3.cloned.1.call-done, bf16[1280,1024]{1,0:T(8,128)(2,1)S(1)} %copy-done), kind=kOutput, calls=%fused_computation.14 | convolution fusion | flops 1342701568 | bytes 4980736 | tf_op jit(solution)/shard_map/dot_general | solution.py:59
  99.1 1.0 copy.50
  100.2 4.1 %copy.52 = bf16[1,1,128,8192]{2,3,1,0:T(8,128)(2,1)} copy(bf16[1,1,128,8192]{3,2,1,0:T(8,128)(2,1)} %param.22) | data formatting | bytes 4194304 | tf_op args[9]
  104.3 4.5 %all-to-all-start.2 = ((bf16[128,4,2048]{0,2,1:T(8,128)(2,1)}), bf16[128,4,2048]{0,2,1:T(8,128)(2,1)}, u32[]{:S(2)}, u32[]{:S(2)}) async-start(bf16[128,4,2048]{0,2,1:T(8,128)(2,1)} %bitcast.55), calls=%async_computation.4 | async-start | bytes 4194304 | tf_op jit(solution)/shard_map/all_to_all | solution.py:43
  109.5 0.7 dynamic_slice.15
  110.2 30.7 %reduce-scatter.6.cloned.1.call-done = bf16[128,1024]{1,0:T(8,128)(2,1)} async-done(((bf16[512,1024]{1,0:T(8,128)(2,1)}), bf16[128,1024]{1,0:T(8,128)(2,1)}) %reduce-scatter.6.cloned.1.call-update) | async-done | bytes 262160 | tf_op jit(solution)/shard_map/reduce_scatter | solution.py:61
  140.8 1.7 add_convert_fusion
  142.5 4.5 %all-to-all-start.1 = ((bf16[8,16,1024]{2,1,0:T(8,128)(2,1)}), bf16[8,16,1024]{2,1,0:T(8,128)(2,1)S(1)}, u32[]{:S(2)}, u32[]{:S(2)}) async-start(bf16[8,16,1024]{2,1,0:T(8,128)(2,1)} %bitcast.13), calls=%async_computation.3 | async-start | bytes 524288 | tf_op jit(solution)/shard_map/all_to_all | solution.py:64
  147.1 3.8 %convert_bitcast_fusion = f32[4,128,2048]{1,2,0:T(8,128)} fusion(bf16[128,4,2048]{0,2,1:T(8,128)(2,1)} %all-to-all-done.2), kind=kLoop, calls=%fused_computation.4 | loop fusion | flops 1048576 | bytes 6291456 | tf_op jit(solution)/shard_map/convert_element_type | solution.py:44
  150.9 5.4 %copy.53 = f32[4,128,2048]{2,1,0:T(8,128)} copy(f32[4,128,2048]{1,2,0:T(8,128)} %convert_bitcast_fusion) | data formatting | bytes 8388608 | tf_op jit(solution)/shard_map/convert_element_type | solution.py:44
  156.8 0.7 copy.54
  157.6 2.7 fusion.1
  160.2 9.2 %convolution_convert_fusion.2 = bf16[512,2048]{1,0:T(8,128)(2,1)} fusion(bf16[512,2048]{1,0:T(8,128)(2,1)S(1)} %fusion.1, bf16[2048,2048]{1,0:T(8,128)(2,1)} %param.24), kind=kOutput, calls=%fused_computation.7 | convolution fusion | flops 4296015872 | bytes 12582912 | tf_op jit(solution)/shard_map/dot_general | solution.py:45
  170.4 13.9 %all-gather.5.cloned.1.call-done = bf16[64,8192]{1,0:T(8,128)(2,1)} async-done(((bf16[16,8192]{1,0:T(8,128)(2,1)}), bf16[64,8192]{1,0:T(8,128)(2,1)}) %all-gather.5.cloned.1.call-update) | async-done | bytes 1048592 | tf_op jit(solution)/shard_map/all_gather | solution.py:65
  184.2 5.8 %convolution_convert_fusion.3 = bf16[64,2048]{1,0:T(8,128)(2,1)} fusion(bf16[2048,2048]{1,0:T(8,128)(2,1)} %param.24, f32[2048]{0:T(1024)S(1)} %dynamic_slice.15, bf16[64,8192]{1,0:T(8,128)(2,1)} %all-gather.5.cloned.1.call-done, s32[]{:T(128)S(6)} %select_n.31), kind=kOutput, calls=%fused_computation.13 | convolution fusion | flops 537395200 | bytes 8921092 | tf_op jit(solution)/shard_map/dot_general | solution.py:69
  190.0 4.2 %multiply_reduce_fusion = (f32[128]{0:T(128)S(1)}, bf16[128,8192]{1,0:T(8,128)(2,1)}) fusion(bf16[1,1,128,8192]{3,2,1,0:T(8,128)(2,1)} %param.22, bf16[64,8192]{1,0:T(8,128)(2,1)} %all-gather.5.cloned.1.call-done, s32[128]{0:T(128)S(1)} %iota_add_fusion, s32[64]{0:T(128)S(1)} %bitcast.66, pred[64]{0:T(512)(128)(4,1)S(1)} %lt.33, pred[128]{0:T(512)(128)(4,1)S(1)} %fusion.23), kind=kOutput, calls=%fused_computation.5 | convolution fusion | flops 139476864 | bytes 5244352 | tf_op jit(solution)/shard_map/dot_general | solution.py:78
  194.2 28.3 %reduce-scatter.8.cloned.1.call-done = bf16[128,2048]{1,0:T(8,128)(2,1)} async-done(((bf16[512,2048]{1,0:T(8,128)(2,1)}), bf16[128,2048]{1,0:T(8,128)(2,1)}) %reduce-scatter.8.cloned.1.call-update) | async-done | bytes 524304 | tf_op jit(solution)/shard_map/reduce_scatter | solution.py:46
  222.5 46.3 %all-reduce.2.cloned.1.call-done = bf16[64,2048]{1,0:T(8,128)(2,1)} async-done(((bf16[64,2048]{1,0:T(8,128)(2,1)}), bf16[64,2048]{1,0:T(8,128)(2,1)}) %all-reduce.2.cloned.1.call-update) | async-done | bytes 262160 | tf_op jit(solution)/shard_map/psum | solution.py:70
  268.9 2.4 fusion.5
  (45 shorter events, 3.1 us)
Async XLA Ops:
  7.2 89.1 %copy-start = (bf16[1280,1024]{1,0:T(8,128)(2,1)S(1)}, bf16[1280,1024]{1,0:T(8,128)(2,1)}, u32[]{:S(2)}) copy-start(bf16[1280,1024]{1,0:T(8,128)(2,1)} %param.20) | copy-start | bytes 7864324
  7.2 65.1 %reduce-scatter.4.cloned.1.call-start = ((), (), s32[]{:S(2)}) async-start(), calls=%async_computation.6 | async-start | bytes 1474560 | tf_op jit(solution)/shard_map/reduce_scatter | solution.py:55
  40.4 55.9 %all-gather.3.cloned.1.call-start = ((), (), s32[]{:S(2)}) async-start(), calls=%async_computation.7 | async-start | bytes 1474560 | tf_op jit(solution)/shard_map/all_gather | solution.py:58
  74.6 66.2 %reduce-scatter.6.cloned.1.call-start = ((), (), s32[]{:S(2)}) async-start(), calls=%async_computation.8 | async-start | bytes 1310720 | tf_op jit(solution)/shard_map/reduce_scatter | solution.py:61
  104.3 38.3 %all-to-all-start.2 = ((bf16[128,4,2048]{0,2,1:T(8,128)(2,1)}), bf16[128,4,2048]{0,2,1:T(8,128)(2,1)}, u32[]{:S(2)}, u32[]{:S(2)}) async-start(bf16[128,4,2048]{0,2,1:T(8,128)(2,1)} %bitcast.55), calls=%async_computation.4 | async-start | bytes 4194304 | tf_op jit(solution)/shard_map/all_to_all | solution.py:43
  142.5 14.2 %all-to-all-start.1 = ((bf16[8,16,1024]{2,1,0:T(8,128)(2,1)}), bf16[8,16,1024]{2,1,0:T(8,128)(2,1)S(1)}, u32[]{:S(2)}, u32[]{:S(2)}) async-start(bf16[8,16,1024]{2,1,0:T(8,128)(2,1)} %bitcast.13), calls=%async_computation.3 | async-start | bytes 524288 | tf_op jit(solution)/shard_map/all_to_all | solution.py:64
  147.0 37.2 %all-gather.5.cloned.1.call-start = ((), (), s32[]{:S(2)}) async-start(), calls=%async_computation.9 | async-start | bytes 1310720 | tf_op jit(solution)/shard_map/all_gather | solution.py:65
  157.5 65.0 %reduce-scatter.8.cloned.1.call-start = ((), (), s32[]{:S(2)}) async-start(), calls=%async_computation.11 | async-start | bytes 2621440 | tf_op jit(solution)/shard_map/reduce_scatter | solution.py:46
  169.4 0.7 copy-start.3
  169.4 0.8 copy-start.1
  169.4 99.4 %all-reduce.2.cloned.1.call-start = ((), (), s32[]{:S(2)}) async-start(), calls=%async_computation.10 | async-start | bytes 524288 | tf_op jit(solution)/shard_map/psum | solution.py:70
  190.0 78.8 %copy-start.2 = (f32[2048]{0:T(1024)S(1)}, f32[2048]{0:T(1024)}, u32[]{:S(2)}) copy-start(f32[2048]{0:T(1024)} %param.25) | copy-start | bytes 24580
Sparse Core Ops, SparseCore 0:
  40.6 31.6 reduce-scatter.3
  74.8 21.5 all-gather.2
  100.3 40.4 reduce-scatter.5
  157.6 26.5 all-gather.4
  187.3 35.1 reduce-scatter.7
  225.9 42.9 all-reduce.1

commit v2 on v1

v2 whole, which is shorter than its diff:
```python
import functools

import jax
import jax.numpy as jnp
from jax import lax
from jax.experimental import pallas as pl
from jax.experimental.pallas import tpu as pltpu
from jax.sharding import PartitionSpec as P

SLOT = 8
F32 = jnp.float32
BF16 = jnp.bfloat16
MESH = pl.DeviceIdType.MESH


def tiles(width, tile):
    return tile if width % tile == 0 else width


def kernel(
    dims,
    patches,
    merge_gain,
    merge_bias,
    up_bias,
    down_bias,
    gain_col,
    kv_bias,
    picks,
    present,
    up_hbm,
    down_hbm,
    kv_hbm,
    text_hbm,
    embedded,
    keys_values,
    up_w,
    down_w,
    kv_w,
    text,
    split,
    rows,
    part,
    pair,
    chip_sum,
    summed,
    hidden,
    lowered,
    low_in,
    vis_part,
    visual,
    vkv,
    vkv_in,
    vkv_all,
    text_cols,
    text_part,
    text_in,
    local_sem,
    send_a,
    recv_a,
    send_b,
    recv_b,
    send_pair,
    recv_pair,
    send_c,
    recv_c,
    send_d,
    recv_d,
    send_fw,
    recv_fw,
    send_e,
    recv_e,
    send_f,
    recv_f,
    send_g,
    recv_g,
    send_h,
    recv_h,
    send_i,
    recv_i,
    send_t,
    recv_t,
    send_u,
    recv_u,
):
    n_enc, n_tp = dims
    groups = 2 * n_enc
    enc, mb, tp = lax.axis_index("enc"), lax.axis_index("mb"), lax.axis_index("tp")
    me = enc * 2 + mb
    own, kw = split.shape[1], split.shape[2]
    units = up_w.shape[1]
    cols = down_w.shape[1]
    feats, kv_cols = kv_w.shape
    tokens = text.shape[0]
    seq_rows = n_tp * own
    per_feat = feats // cols

    def other_groups():
        for step in range(1, groups):
            to = lax.rem(me + step, groups)
            yield to, {"enc": lax.div(to, 2), "mb": lax.rem(to, 2)}

    def other_encs():
        for step in range(1, n_enc):
            to = lax.rem(enc + step, n_enc)
            yield to, {"enc": to}

    def other_tps():
        for step in range(1, n_tp):
            to = lax.rem(tp + step, n_tp)
            yield to, {"tp": to}

    mate = {"mb": 1 - mb}

    def remote(src, dst, send, recv, to):
        return pltpu.make_async_remote_copy(
            src_ref=src, dst_ref=dst, send_sem=send, recv_sem=recv, device_id=to, device_id_type=MESH
        )

    local = [
        pltpu.make_async_copy(src, dst, local_sem.at[i])
        for i, (src, dst) in enumerate(
            ((up_hbm, up_w), (down_hbm, down_w), (kv_hbm, kv_w), (text_hbm, text))
        )
    ]
    for copy in local:
        copy.start()

    barrier = pltpu.get_barrier_semaphore()
    for _, to in other_groups():
        pl.semaphore_signal(barrier, inc=1, device_id=to, device_id_type=MESH)
    for _, to in other_tps():
        pl.semaphore_signal(barrier, inc=1, device_id=to, device_id_type=MESH)

    gain, bias = merge_gain[...], merge_bias[...]
    width = patches.shape[2]
    for j in range(4):
        values = patches[j].astype(F32)
        center = values - jnp.mean(values, axis=-1, keepdims=True)
        spread = jnp.mean(center * center, axis=-1, keepdims=True)
        normal = (center * lax.rsqrt(spread + 1e-06) * gain + bias).astype(BF16)
        for piece in range(width // kw):
            split[j * (width // kw) + piece] = normal[:, piece * kw : (piece + 1) * kw]
    pl.semaphore_wait(barrier, groups - 1 + n_tp - 1)

    copies_a = []
    for to, where in other_groups():
        copy = remote(split.at[to], rows.at[me, tp], send_a.at[to], recv_a.at[me], where)
        copy.start()
        copies_a.append(copy)
    rows[me, tp] = split[me]
    for at, where in other_groups():
        remote(split.at[at], rows.at[at, tp], send_a.at[at], recv_a.at[at], where).wait_recv()
    copies_b = []
    for to, where in other_tps():
        copy = remote(rows.at[:, tp], rows.at[:, tp], send_b.at[to], recv_b.at[tp], where)
        copy.start()
        copies_b.append(copy)

    copies_t = []
    for to, where in other_tps():
        copy = remote(
            text_hbm.at[:, pl.ds(pl.multiple_of(to * feats, feats), feats)],
            text_cols.at[tp],
            send_t.at[to],
            recv_t.at[tp],
            where,
        )
        copy.start()
        copies_t.append(copy)

    local[0].wait()
    for at, where in other_tps():
        remote(rows.at[:, at], rows.at[:, at], send_b.at[at], recv_b.at[at], where).wait_recv()

    tile = tiles(units, 256)

    @pl.loop(0, units // tile)
    def _(i):
        at = pl.ds(pl.multiple_of(i * tile, tile), tile)
        lhs = rows[...].reshape(groups * seq_rows, kw)
        out = jnp.dot(lhs, up_w[:, at], preferred_element_type=F32)
        part[:, :, :, at] = out.astype(BF16).reshape(n_enc, 2, seq_rows, tile)

    to_pair = remote(part.at[:, 1 - mb], pair, send_pair, recv_pair, mate)
    to_pair.start()
    to_pair.wait_recv()
    copies_c = []
    for to, where in other_encs():
        chip_sum[to] = (part[to, mb].astype(F32) + pair[to].astype(F32)).astype(BF16)
        copy = remote(chip_sum.at[to], summed.at[enc], send_c.at[to], recv_c.at[enc], where)
        copy.start()
        copies_c.append(copy)

    local[2].wait()

    @pl.loop(0, feats // 128)
    def _(i):
        at = pl.ds(pl.multiple_of(i * 128, 128), 128)
        kv_w[at, :] = (kv_w[at, :].astype(F32) * gain_col[at, :]).astype(BF16)

    local[3].wait()
    text_cols[tp] = text[:, pl.ds(pl.multiple_of(tp * feats, feats), feats)]

    total = part[enc, mb].astype(F32) + pair[enc].astype(F32) + up_bias[...]
    for at, where in other_encs():
        remote(chip_sum.at[at], summed.at[at], send_c.at[at], recv_c.at[at], where).wait_recv()
        total = total + summed[at].astype(F32)
    hidden[enc, mb] = (0.5 * total * (1.0 + lax.erf(total * 0.7071067811865476))).astype(BF16)

    copies_d = []
    copy = remote(hidden.at[enc, mb], hidden.at[enc, mb], send_fw.at[enc], recv_fw.at[enc], mate)
    copy.start()
    copies_d.append(copy)
    for to, where in other_encs():
        copy = remote(hidden.at[enc, mb], hidden.at[enc, mb], send_d.at[to], recv_d.at[enc], where)
        copy.start()
        copies_d.append(copy)

    for at, where in other_tps():
        remote(text_cols.at[at], text_cols.at[at], send_t.at[at], recv_t.at[at], where).wait_recv()
    tile = tiles(kv_cols, 256)

    @pl.loop(0, kv_cols // tile)
    def _(i):
        at = pl.ds(pl.multiple_of(i * tile, tile), tile)
        lhs = text_cols[...].reshape(n_tp * tokens, feats)
        out = jnp.dot(lhs, kv_w[:, at], preferred_element_type=F32)
        text_part[:, :, at] = out.astype(BF16).reshape(n_tp, tokens, tile)

    copies_u = []
    for to, where in other_tps():
        copy = remote(text_part.at[to], text_in.at[tp], send_u.at[to], recv_u.at[tp], where)
        copy.start()
        copies_u.append(copy)

    for at, where in other_encs():
        remote(hidden.at[at, mb], hidden.at[at, mb], send_d.at[at], recv_d.at[at], where).wait_recv()
        copy = remote(hidden.at[at, mb], hidden.at[at, mb], send_fw.at[at], recv_fw.at[at], mate)
        copy.start()
        copies_d.append(copy)
    for at in range(n_enc):
        remote(
            hidden.at[at, 1 - mb], hidden.at[at, 1 - mb], send_fw.at[at], recv_fw.at[at], mate
        ).wait_recv()

    local[1].wait()
    tile = tiles(cols, 256)

    @pl.loop(0, cols // tile)
    def _(i):
        at = pl.ds(pl.multiple_of(i * tile, tile), tile)
        lhs = hidden[...].reshape(groups * seq_rows, units)
        out = jnp.dot(lhs, down_w[:, at], preferred_element_type=F32)
        lowered[:, :, :, at] = out.astype(BF16).reshape(groups, n_tp, own, tile)

    copies_e = []
    for to, where in other_tps():
        copy = remote(lowered.at[:, to], low_in.at[tp], send_e.at[to], recv_e.at[tp], where)
        copy.start()
        copies_e.append(copy)
    for at, where in other_tps():
        remote(lowered.at[:, at], low_in.at[at], send_e.at[at], recv_e.at[at], where).wait_recv()
    low_in[tp] = lowered[:, tp]
    copies_f = []

    def finish(to):
        out = down_bias[...] + jnp.zeros((own, cols), F32)
        for t in range(n_tp):
            out = out + low_in[t, to].astype(F32)
        vis_part[to] = out.astype(BF16)

    for to, where in other_groups():
        finish(to)
        copy = remote(vis_part.at[to], visual.at[tp, me], send_f.at[to], recv_f.at[me], where)
        copy.start()
        copies_f.append(copy)
    finish(me)
    visual[tp, me] = vis_part[me]
    for at, where in other_groups():
        remote(vis_part.at[at], visual.at[tp, at], send_f.at[at], recv_f.at[at], where).wait_recv()
    copies_g = []
    for to, where in other_tps():
        copy = remote(visual.at[tp], visual.at[tp], send_g.at[to], recv_g.at[tp], where)
        copy.start()
        copies_g.append(copy)
    for at, where in other_tps():
        remote(visual.at[at], visual.at[at], send_g.at[at], recv_g.at[at], where).wait_recv()

    tile = tiles(kv_cols, 512)

    @pl.loop(0, kv_cols // tile)
    def _(i):
        at = pl.ds(pl.multiple_of(i * tile, tile), tile)
        out = jnp.zeros((seq_rows, tile), F32)
        for j in range(per_feat):
            lhs = visual[:, tp * per_feat + j].reshape(seq_rows, cols)
            out = out + jnp.dot(lhs, kv_w[j * cols : (j + 1) * cols, at], preferred_element_type=F32)
        vkv[:, :, at] = out.astype(BF16).reshape(n_tp, own, tile)

    copies_h = []
    for to, where in other_tps():
        copy = remote(vkv.at[to], vkv_in.at[tp], send_h.at[to], recv_h.at[tp], where)
        copy.start()
        copies_h.append(copy)
    vkv_in[tp] = vkv[tp]
    for at, where in other_tps():
        remote(vkv.at[at], vkv_in.at[at], send_h.at[at], recv_h.at[at], where).wait_recv()
    out = vkv_in[0].astype(F32)
    for t in range(1, n_tp):
        out = out + vkv_in[t].astype(F32)
    vkv_all[tp] = out.astype(BF16)
    copies_i = []
    for to, where in other_tps():
        copy = remote(vkv_all.at[tp], vkv_all.at[tp], send_i.at[to], recv_i.at[tp], where)
        copy.start()
        copies_i.append(copy)

    def place(i, squares):
        at = pl.ds(pl.multiple_of(i * cols, cols), cols)
        found = jnp.dot(
            picks[...], visual[:, i].reshape(seq_rows, cols), preferred_element_type=F32
        ).astype(BF16).astype(F32)
        mask = jnp.broadcast_to(present[...], (tokens, cols)) > 0
        values = jnp.where(mask, found, text[:, at].astype(F32))
        embedded[:, at] = values.astype(BF16)
        return squares + jnp.sum(values * values, axis=-1, keepdims=True)

    squares = lax.fori_loop(0, groups, place, jnp.zeros((tokens, 1), F32))
    scale = lax.rsqrt(squares * (1.0 / (groups * cols)) + 1e-06)

    text_in[tp] = text_part[tp]
    for at, where in other_tps():
        remote(text_part.at[at], text_in.at[at], send_u.at[at], recv_u.at[at], where).wait_recv()
    for at, where in other_tps():
        remote(vkv_all.at[at], vkv_all.at[at], send_i.at[at], recv_i.at[at], where).wait_recv()

    @pl.loop(0, kv_cols // tile)
    def _(i):
        at = pl.ds(pl.multiple_of(i * tile, tile), tile)
        found = jnp.dot(
            picks[...], vkv_all[:, :, at].reshape(seq_rows, tile), preferred_element_type=F32
        )
        plain = text_in[0, :, at].astype(F32)
        for t in range(1, n_tp):
            plain = plain + text_in[t, :, at].astype(F32)
        mask = jnp.broadcast_to(present[...], (tokens, tile)) > 0
        keys_values[:, at] = (jnp.where(mask, found, plain) * scale + kv_bias[:, at]).astype(BF16)

    to_pair.wait_send()
    for copies in (
        copies_a, copies_b, copies_t, copies_c, copies_d, copies_u,
        copies_e, copies_f, copies_g, copies_h, copies_i,
    ):
        for copy in copies:
            copy.wait_send()


def per_device(
    patches,
    patch_counts,
    dest_pos,
    merge_gain,
    merge_bias,
    up_weight,
    up_bias,
    down_weight,
    down_bias,
    text_embed,
    norm_gain,
    kv_weight,
    kv_bias,
):
    n_enc, n_tp = lax.axis_size("enc"), lax.axis_size("tp")
    groups = n_enc * lax.axis_size("mb")
    tp = lax.axis_index("tp")
    group = lax.axis_index("enc") * lax.axis_size("mb") + lax.axis_index("mb")
    text = text_embed[0, 0]
    tokens, width = text.shape
    feats, kv_cols = kv_weight.shape
    kw, units = up_weight.shape
    cols = down_weight.shape[1]
    own = patches.shape[2] // 4
    seq_rows = own * n_tp

    live_rows = patch_counts[0, 0] // 4
    live = (jnp.arange(SLOT, dtype=jnp.int32)[None, :] < live_rows[:, None]).reshape(-1)
    places = tp * tokens + jnp.arange(tokens, dtype=jnp.int32)
    select = (dest_pos[0, 0][None, :] == places[:, None]) & live[None, :]
    picks = select.astype(BF16)
    present = jnp.any(select, axis=1)[:, None].astype(jnp.int32)
    by_piece = patches[0, 0].reshape(own, 4, patches.shape[3]).transpose(1, 0, 2)

    dma = pltpu.SemaphoreType.DMA
    vmem = pl.BlockSpec(memory_space=pltpu.VMEM)
    hbm = pl.BlockSpec(memory_space=pl.ANY)
    by_group, by_enc, by_tp = [dma((groups,))] * 2, [dma((n_enc,))] * 2, [dma((n_tp,))] * 2
    embedded, keys_values = pl.pallas_call(
        functools.partial(kernel, (n_enc, n_tp)),
        out_shape=(
            jax.ShapeDtypeStruct((tokens, width), BF16),
            jax.ShapeDtypeStruct((tokens, kv_cols), BF16),
        ),
        in_specs=[vmem] * 9 + [hbm] * 4,
        out_specs=(vmem, vmem),
        scratch_shapes=[
            pltpu.VMEM((kw, units), BF16),
            pltpu.VMEM((units, cols), BF16),
            pltpu.VMEM((feats, kv_cols), BF16),
            pltpu.VMEM((tokens, width), BF16),
            pltpu.VMEM((groups, own, kw), BF16),
            pltpu.VMEM((groups, n_tp, own, kw), BF16),
            pltpu.VMEM((n_enc, 2, seq_rows, units), BF16),
            pltpu.VMEM((n_enc, seq_rows, units), BF16),
            pltpu.VMEM((n_enc, seq_rows, units), BF16),
            pltpu.VMEM((n_enc, seq_rows, units), BF16),
            pltpu.VMEM((n_enc, 2, seq_rows, units), BF16),
            pltpu.VMEM((groups, n_tp, own, cols), BF16),
            pltpu.VMEM((n_tp, groups, own, cols), BF16),
            pltpu.VMEM((groups, own, cols), BF16),
            pltpu.VMEM((n_tp, groups, own, cols), BF16),
            pltpu.VMEM((n_tp, own, kv_cols), BF16),
            pltpu.VMEM((n_tp, own, kv_cols), BF16),
            pltpu.VMEM((n_tp, own, kv_cols), BF16),
            pltpu.VMEM((n_tp, tokens, feats), BF16),
            pltpu.VMEM((n_tp, tokens, kv_cols), BF16),
            pltpu.VMEM((n_tp, tokens, kv_cols), BF16),
            dma((4,)),
        ]
        + by_group + by_tp + [dma, dma] + by_enc + by_enc + by_enc
        + by_tp + by_group + by_tp + by_tp + by_tp + by_tp + by_tp,
        compiler_params=pltpu.CompilerParams(
            collective_id=0, has_side_effects=True, vmem_limit_bytes=60 * 1024 * 1024
        ),
        cost_estimate=pl.CostEstimate(
            flops=2 * groups * seq_rows * units * (kw + cols) + 2 * n_tp * tokens * feats * kv_cols,
            bytes_accessed=2 * (kw * units + units * cols + feats * kv_cols + 2 * tokens * width),
            transcendentals=seq_rows * units,
        ),
    )(
        by_piece,
        merge_gain[None],
        merge_bias[None],
        lax.dynamic_slice_in_dim(up_bias, tp * units, units, 0)[None],
        lax.dynamic_slice_in_dim(down_bias, group * cols, cols, 0)[None],
        lax.dynamic_slice_in_dim(norm_gain, tp * feats, feats, 0)[:, None],
        kv_bias[None],
        picks,
        present,
        up_weight,
        down_weight,
        kv_weight,
        text,
    )
    return (embedded[None, None], keys_values[None, None])


def solution(mesh):
    return jax.shard_map(
        per_device,
        mesh=mesh,
        in_specs=(
            P("enc", "mb", "tp", None),
            P("enc", "mb", None),
            P("enc", "mb", None),
            P(),
            P(),
            P(("enc", "mb"), "tp"),
            P(),
            P("tp", ("enc", "mb")),
            P(),
            P("enc", "mb", "tp", None),
            P(),
            P("tp", None),
            P(),
        ),
        out_specs=(P("enc", "mb", "tp", None), P("enc", "mb", "tp", None)),
        check_vma=False,
    )
```

time: 279 us -> 136 us (0.49)
  waiting for transfers between devices: 172 us -> 0 us
  Pallas kernels: 0 us -> 119 us
  matrix products: 26.9 us -> 0 us
  blocking collectives: 23.9 us -> 0 us
  between operations: 14.3 us -> 0.67 us
  other arithmetic: 13.1 us -> 2.11 us
  starting transfers between devices: 9.17 us -> 0 us
  local copies, waits for them, and re-layouts: 18.2 us -> 13.7 us
    pallas_call x0 -> x1, Pallas kernels: none -> 119 us  [per_device(): pl.pallas_call(functools.partial(kernel, (n_enc, n_tp)), out_shape=(jax.S...]
    reduce_scatter x3 -> x0, waiting for transfers between devices: 90 us -> none  [the longest x1 31 us: per_device(): lax.psum_scatter(raised, GROUP, scatter_dimension=0, tiled=True)]
    psum x1 -> x0, waiting for transfers between devices: 46.3 us -> none  [per_device(): visual_kv = lax.psum(visual_part, 'tp')]
    all_gather x2 -> x0, waiting for transfers between devices: 35.5 us -> none  [the longest x1 21.6 us: per_device(): all_hidden = lax.all_gather(hidden, GROUP, axis=0, tiled=True)]
    dot_general x6 -> x0, matrix products: 27 us -> none  [the longest x1 9.18 us: per_device(): jnp.dot(scaled, kv_weight, preferred_element_type=jnp.float32)]
    all_to_all x1 -> x0, blocking collectives: 13.3 us -> none  [per_device(): lax.all_to_all(merged, GROUP, split_axis=1, concat_axis=0, tiled=True)]
    convert_element_type x5 -> x1, other arithmetic: 10.6 us -> 0.01 us  [per_device(): present = jnp.any(select, axis=1)[:, None].astype(jnp.int32)]
    all_gather x1 -> x0, blocking collectives: 10.6 us -> none  [per_device(): rows = lax.all_gather(slices, 'tp', axis=0, tiled=True)]
  transfers between devices with their start and end apart: 8 -> 0, of which waited for: 7 -> 0; matrix products, arithmetic and copies ran while one was open for 14% -> 0% of each run, Pallas kernels for 0% -> 0%
where the time goes in v2:
time: 136 us; the launch traced here: 135 us
  Pallas kernels  119 us (88%)
  local copies, waits for them, and re-layouts  13.7 us (10%)
  other arithmetic  2.11 us (2%)
    pallas_call x1, Pallas kernels, per_device(): pl.pallas_call(functools.partial(kernel, (n_enc, n_tp)), out_shape=(jax.S...  119 us
    unnamed x4, local copies, waits for them, and re-layouts  3.95 us

profile of v2, /device:TPU:0, one launch (start us, length us, event | category | flops | bytes accessed | tf_op | source)
XLA Modules:
  0.0 135.5 jit_solution(15415776614105062541)
XLA Ops:
  0.6 0.7 and_select_fusion
  1.3 0.1 iota_compare_fusion
  1.4 0.1 lt.35
  1.5 1.3 dynamic_slice.10
  2.8 1.3 broadcast_in_dim.28.merge_gain
  4.1 1.3 broadcast_in_dim.29.merge_bias
  5.3 0.8 dynamic_slice.9
  6.1 0.6 broadcast_in_dim.30.up_bias
  6.7 0.7 dynamic_slice.11
  7.4 1.4 %fusion = (pred[128]{0:T(512)(128)(4,1)S(1)}, bf16[128,64]{1,0:T(8,128)(2,1)}) fusion(s32[64]{0:T(128)} %bitcast.27, s32[128]{0:T(128)S(1)} %iota_add_fusion, pred[64]{0:T(512)(128)(4,1)S(1)} %lt.35), kind=kLoop, calls=%fused_computation.2 | loop fusion | flops 32640 | bytes 17344 | tf_op jit(solution)/shard_map/reduce_or | solution.py:391
  8.8 0.7 copy.18.present
  9.5 1.0 reshape_squeeze.3
  10.5 0.7 copy.20
  11.2 1.3 copy.17.gain_col
  12.5 119.0 %shard_map.140 = (bf16[128,8192]{1,0:T(8,128)(2,1)}, bf16[128,2048]{1,0:T(8,128)(2,1)}) custom-call(bf16[4,16,1280]{2,1,0:T(8,128)(2,1)} %bitcast.24, f32[1,1280]{1,0:T(1,128)} %broadcast_in_dim.28.merge_gain, f32[1,1280]{1,0:T(1,128)} %broadcast_in_dim.29.merge_bias, f32[1,1280]{1,0:T(1,128)} %broadcast_in_dim.30.up_bias, f32[1,1024]{1,0:T(1,128)} %bitcast.26, ...), custom_call_target="tpu_custom_call" | custom-call | flops 6476005376 | bytes 16842752 | tf_op jit(solution)/shard_map/pallas_call | solution.py:398
  131.5 0.0 copy-start
  131.5 3.2 %copy.23 = bf16[1,1,128,8192]{3,2,1,0:T(8,128)(2,1)} copy(bf16[1,1,128,8192]{3,2,1,0:T(8,128)(2,1)} %bitcast.22) | data formatting | bytes 4194304
  134.7 0.0 copy-done
  134.7 0.8 copy.24
  (2 shorter events, 0.0 us)
Async XLA Ops:
  131.5 3.2 %copy-start = (bf16[128,2048]{1,0:T(8,128)(2,1)S(1)}, bf16[128,2048]{1,0:T(8,128)(2,1)}, u32[]{:S(2)}) copy-start(bf16[128,2048]{1,0:T(8,128)(2,1)} %get-tuple-element.5) | copy-start | bytes 1572868

commit v3 on v2

--- a/solution.py
+++ b/solution.py
@@ -20,14 +20,8 @@
 def kernel(
     dims,
     patches,
-    merge_gain,
-    merge_bias,
-    up_bias,
-    down_bias,
-    gain_col,
-    kv_bias,
-    picks,
-    present,
+    params,
+    dest,
     up_hbm,
     down_hbm,
     kv_hbm,
@@ -55,6 +49,8 @@
     text_cols,
     text_part,
     text_in,
+    picks,
+    present,
     local_sem,
     send_a,
     recv_a,
@@ -88,12 +84,19 @@
     enc, mb, tp = lax.axis_index("enc"), lax.axis_index("mb"), lax.axis_index("tp")
     me = enc * 2 + mb
     own, kw = split.shape[1], split.shape[2]
+    width = patches.shape[1]
     units = up_w.shape[1]
     cols = down_w.shape[1]
     feats, kv_cols = kv_w.shape
     tokens = text.shape[0]
     seq_rows = n_tp * own
     per_feat = feats // cols
+    cuts = [0]
+    for size in (width, width, kv_cols, feats, cols, units):
+        cuts.append(cuts[-1] + size)
+    merge_gain, merge_bias, kv_bias, norm_gain, down_bias, up_bias = (
+        params.at[:, start:stop] for start, stop in zip(cuts[:-1], cuts[1:])
+    )
 
     def other_groups():
         for step in range(1, groups):
@@ -132,30 +135,40 @@
     for _, to in other_tps():
         pl.semaphore_signal(barrier, inc=1, device_id=to, device_id_type=MESH)
 
-    gain, bias = merge_gain[...], merge_bias[...]
-    width = patches.shape[2]
+    values = patches[...].astype(F32)
+    center = values - jnp.mean(values, axis=-1, keepdims=True)
+    spread = jnp.mean(center * center, axis=-1, keepdims=True)
+    normal = (center * lax.rsqrt(spread + 1e-06) * merge_gain[...] + merge_bias[...]).astype(BF16)
+    row = lax.broadcasted_iota(jnp.int32, (own, 4 * own), 0)
+    column = lax.broadcasted_iota(jnp.int32, (own, 4 * own), 1)
     for j in range(4):
-        values = patches[j].astype(F32)
-        center = values - jnp.mean(values, axis=-1, keepdims=True)
-        spread = jnp.mean(center * center, axis=-1, keepdims=True)
-        normal = (center * lax.rsqrt(spread + 1e-06) * gain + bias).astype(BF16)
+        chosen = jnp.where(column == 4 * row + j, 1.0, 0.0).astype(BF16)
+        every = jnp.dot(chosen, normal, preferred_element_type=F32).astype(BF16)
         for piece in range(width // kw):
-            split[j * (width // kw) + piece] = normal[:, piece * kw : (piece + 1) * kw]
+            split[j * (width // kw) + piece] = every[:, piece * kw : (piece + 1) * kw]
+    place_of = lax.broadcasted_iota(jnp.int32, (tokens, seq_rows), 0)
+    chosen = jnp.where(place_of == dest[...], 1.0, 0.0)
+    picks[...] = chosen.astype(BF16)
+    present[...] = jnp.sum(chosen, axis=-1, keepdims=True)
     pl.semaphore_wait(barrier, groups - 1 + n_tp - 1)
 
     copies_a = []
     for to, where in other_groups():
-        copy = remote(split.at[to], rows.at[me, tp], send_a.at[to], recv_a.at[me], where)
+        copy = remote(split.at[to], rows.at[enc, mb, tp], send_a.at[to], recv_a.at[me], where)
         copy.start()
         copies_a.append(copy)
-    rows[me, tp] = split[me]
+    rows[enc, mb, tp] = split[me]
     for at, where in other_groups():
-        remote(split.at[at], rows.at[at, tp], send_a.at[at], recv_a.at[at], where).wait_recv()
+        remote(split.at[at], rows.at[lax.div(at, 2), lax.rem(at, 2), tp], send_a.at[at], recv_a.at[at], where).wait_recv()
     copies_b = []
     for to, where in other_tps():
-        copy = remote(rows.at[:, tp], rows.at[:, tp], send_b.at[to], recv_b.at[tp], where)
+        copy = remote(rows.at[:, :, tp], rows.at[:, :, tp], send_b.at[to], recv_b.at[tp], where)
         copy.start()
         copies_b.append(copy)
+
+    local[0].wait()
+    for at, where in other_tps():
+        remote(rows.at[:, :, at], rows.at[:, :, at], send_b.at[at], recv_b.at[at], where).wait_recv()
 
     copies_t = []
     for to, where in other_tps():
@@ -169,21 +182,20 @@
         copy.start()
         copies_t.append(copy)
 
-    local[0].wait()
-    for at, where in other_tps():
-        remote(rows.at[:, at], rows.at[:, at], send_b.at[at], recv_b.at[at], where).wait_recv()
-
     tile = tiles(units, 256)
 
-    @pl.loop(0, units // tile)
-    def _(i):
-        at = pl.ds(pl.multiple_of(i * tile, tile), tile)
-        lhs = rows[...].reshape(groups * seq_rows, kw)
-        out = jnp.dot(lhs, up_w[:, at], preferred_element_type=F32)
-        part[:, :, :, at] = out.astype(BF16).reshape(n_enc, 2, seq_rows, tile)
-
+    def raise_half(half):
+        @pl.loop(0, units // tile)
+        def _(i):
+            at = pl.ds(pl.multiple_of(i * tile, tile), tile)
+            lhs = rows[:, half].reshape(n_enc * seq_rows, kw)
+            out = jnp.dot(lhs, up_w[:, at], preferred_element_type=F32)
+            part[:, half, :, at] = out.astype(BF16).reshape(n_enc, seq_rows, tile)
+
+    raise_half(1 - mb)
     to_pair = remote(part.at[:, 1 - mb], pair, send_pair, recv_pair, mate)
     to_pair.start()
+    raise_half(mb)
     to_pair.wait_recv()
     copies_c = []
     for to, where in other_encs():
@@ -191,13 +203,6 @@
         copy = remote(chip_sum.at[to], summed.at[enc], send_c.at[to], recv_c.at[enc], where)
         copy.start()
         copies_c.append(copy)
-
-    local[2].wait()
-
-    @pl.loop(0, feats // 128)
-    def _(i):
-        at = pl.ds(pl.multiple_of(i * 128, 128), 128)
-        kv_w[at, :] = (kv_w[at, :].astype(F32) * gain_col[at, :]).astype(BF16)
 
     local[3].wait()
     text_cols[tp] = text[:, pl.ds(pl.multiple_of(tp * feats, feats), feats)]
@@ -219,6 +224,9 @@
 
     for at, where in other_tps():
         remote(text_cols.at[at], text_cols.at[at], send_t.at[at], recv_t.at[at], where).wait_recv()
+    local[2].wait()
+    for at in range(n_tp):
+        text_cols[at] = (text_cols[at].astype(F32) * norm_gain[...]).astype(BF16)
     tile = tiles(kv_cols, 256)
 
     @pl.loop(0, kv_cols // tile)
@@ -228,11 +236,23 @@
         out = jnp.dot(lhs, kv_w[:, at], preferred_element_type=F32)
         text_part[:, :, at] = out.astype(BF16).reshape(n_tp, tokens, tile)
 
+    half = kv_cols // 2
+
+    def text_piece(h, src, dst, to, where):
+        at = pl.ds(h * half, half)
+        return remote(
+            text_part.at[src, :, at], text_in.at[dst, :, at], send_u.at[h, to], recv_u.at[h, dst], where
+        )
+
     copies_u = []
-    for to, where in other_tps():
-        copy = remote(text_part.at[to], text_in.at[tp], send_u.at[to], recv_u.at[tp], where)
-        copy.start()
-        copies_u.append(copy)
+
+    def send_text(h):
+        for to, where in other_tps():
+            copy = text_piece(h, to, tp, to, where)
+            copy.start()
+            copies_u.append(copy)
+
+    send_text(0)
 
     for at, where in other_encs():
         remote(hidden.at[at, mb], hidden.at[at, mb], send_d.at[at], recv_d.at[at], where).wait_recv()
@@ -261,6 +281,7 @@
         copies_e.append(copy)
     for at, where in other_tps():
         remote(lowered.at[:, at], low_in.at[at], send_e.at[at], recv_e.at[at], where).wait_recv()
+    send_text(1)
     low_in[tp] = lowered[:, tp]
     copies_f = []
 
@@ -279,13 +300,20 @@
     visual[tp, me] = vis_part[me]
     for at, where in other_groups():
         remote(vis_part.at[at], visual.at[tp, at], send_f.at[at], recv_f.at[at], where).wait_recv()
-    copies_g = []
-    for to, where in other_tps():
-        copy = remote(visual.at[tp], visual.at[tp], send_g.at[to], recv_g.at[tp], where)
-        copy.start()
-        copies_g.append(copy)
-    for at, where in other_tps():
-        remote(visual.at[at], visual.at[at], send_g.at[at], recv_g.at[at], where).wait_recv()
+
+    def visual_piece(of, block, to, where):
+        at = visual.at[of, pl.ds(block * per_feat, per_feat)]
+        return remote(at, at, send_g.at[to, block], recv_g.at[of, block], where)
+
+    for to, where in other_tps():
+        visual_piece(tp, to, to, where).start()
+    for at, where in other_tps():
+        visual_piece(at, tp, at, where).wait_recv()
+    for to, where in other_tps():
+
+        @pl.loop(1, n_tp)
+        def _(step):
+            visual_piece(tp, lax.rem(to + step, n_tp), to, where).start()
 
     tile = tiles(kv_cols, 512)
 
@@ -294,7 +322,9 @@
         at = pl.ds(pl.multiple_of(i * tile, tile), tile)
         out = jnp.zeros((seq_rows, tile), F32)
         for j in range(per_feat):
+            gain = norm_gain[:, j * cols : (j + 1) * cols]
             lhs = visual[:, tp * per_feat + j].reshape(seq_rows, cols)
+            lhs = (lhs.astype(F32) * gain).astype(BF16)
             out = out + jnp.dot(lhs, kv_w[j * cols : (j + 1) * cols, at], preferred_element_type=F32)
         vkv[:, :, at] = out.astype(BF16).reshape(n_tp, own, tile)
 
@@ -316,12 +346,18 @@
         copy.start()
         copies_i.append(copy)
 
+    for at, where in other_tps():
+
+        @pl.loop(1, n_tp)
+        def _(step):
+            visual_piece(at, lax.rem(tp + step, n_tp), at, where).wait_recv()
+
     def place(i, squares):
         at = pl.ds(pl.multiple_of(i * cols, cols), cols)
         found = jnp.dot(
             picks[...], visual[:, i].reshape(seq_rows, cols), preferred_element_type=F32
         ).astype(BF16).astype(F32)
-        mask = jnp.broadcast_to(present[...], (tokens, cols)) > 0
+        mask = jnp.broadcast_to(present[...], (tokens, cols)) > 0.5
         values = jnp.where(mask, found, text[:, at].astype(F32))
         embedded[:, at] = values.astype(BF16)
         return squares + jnp.sum(values * values, axis=-1, keepdims=True)
@@ -331,7 +367,8 @@
 
     text_in[tp] = text_part[tp]
     for at, where in other_tps():
-        remote(text_part.at[at], text_in.at[at], send_u.at[at], recv_u.at[at], where).wait_recv()
+        for h in range(2):
+            text_piece(h, at, at, at, where).wait_recv()
     for at, where in other_tps():
         remote(vkv_all.at[at], vkv_all.at[at], send_i.at[at], recv_i.at[at], where).wait_recv()
 
@@ -344,16 +381,21 @@
         plain = text_in[0, :, at].astype(F32)
         for t in range(1, n_tp):
             plain = plain + text_in[t, :, at].astype(F32)
-        mask = jnp.broadcast_to(present[...], (tokens, tile)) > 0
+        mask = jnp.broadcast_to(present[...], (tokens, tile)) > 0.5
         keys_values[:, at] = (jnp.where(mask, found, plain) * scale + kv_bias[:, at]).astype(BF16)
 
     to_pair.wait_send()
     for copies in (
         copies_a, copies_b, copies_t, copies_c, copies_d, copies_u,
-        copies_e, copies_f, copies_g, copies_h, copies_i,
+        copies_e, copies_f, copies_h, copies_i,
     ):
         for copy in copies:
             copy.wait_send()
+    for to, where in other_tps():
+
+        @pl.loop(0, n_tp)
+        def _(block):
+            visual_piece(tp, block, to, where).wait_send()
 
 
 def per_device(
@@ -385,11 +427,17 @@
 
     live_rows = patch_counts[0, 0] // 4
     live = (jnp.arange(SLOT, dtype=jnp.int32)[None, :] < live_rows[:, None]).reshape(-1)
-    places = tp * tokens + jnp.arange(tokens, dtype=jnp.int32)
-    select = (dest_pos[0, 0][None, :] == places[:, None]) & live[None, :]
-    picks = select.astype(BF16)
-    present = jnp.any(select, axis=1)[:, None].astype(jnp.int32)
-    by_piece = patches[0, 0].reshape(own, 4, patches.shape[3]).transpose(1, 0, 2)
+    dest = (jnp.where(live, dest_pos[0, 0], -1) - tp * tokens)[None]
+    params = jnp.concatenate(
+        [
+            merge_gain,
+            merge_bias,
+            kv_bias,
+            lax.dynamic_slice_in_dim(norm_gain, tp * feats, feats, 0),
+            lax.dynamic_slice_in_dim(down_bias, group * cols, cols, 0),
+            lax.dynamic_slice_in_dim(up_bias, tp * units, units, 0),
+        ]
+    )[None]
 
     dma = pltpu.SemaphoreType.DMA
     vmem = pl.BlockSpec(memory_space=pltpu.VMEM)
@@ -401,7 +449,7 @@
             jax.ShapeDtypeStruct((tokens, width), BF16),
             jax.ShapeDtypeStruct((tokens, kv_cols), BF16),
         ),
-        in_specs=[vmem] * 9 + [hbm] * 4,
+        in_specs=[vmem] * 3 + [hbm] * 4,
         out_specs=(vmem, vmem),
         scratch_shapes=[
             pltpu.VMEM((kw, units), BF16),
@@ -409,7 +457,7 @@
             pltpu.VMEM((feats, kv_cols), BF16),
             pltpu.VMEM((tokens, width), BF16),
             pltpu.VMEM((groups, own, kw), BF16),
-            pltpu.VMEM((groups, n_tp, own, kw), BF16),
+            pltpu.VMEM((n_enc, 2, n_tp, own, kw), BF16),
             pltpu.VMEM((n_enc, 2, seq_rows, units), BF16),
             pltpu.VMEM((n_enc, seq_rows, units), BF16),
             pltpu.VMEM((n_enc, seq_rows, units), BF16),
@@ -425,10 +473,12 @@
             pltpu.VMEM((n_tp, tokens, feats), BF16),
             pltpu.VMEM((n_tp, tokens, kv_cols), BF16),
             pltpu.VMEM((n_tp, tokens, kv_cols), BF16),
+            pltpu.VMEM((tokens, seq_rows), BF16),
+            pltpu.VMEM((tokens, 1), F32),
             dma((4,)),
         ]
         + by_group + by_tp + [dma, dma] + by_enc + by_enc + by_enc
-        + by_tp + by_group + by_tp + by_tp + by_tp + by_tp + by_tp,
+        + by_tp + by_group + [dma((n_tp, n_tp))] * 2 + by_tp + by_tp + by_tp + [dma((2, n_tp))] * 2,
         compiler_params=pltpu.CompilerParams(
             collective_id=0, has_side_effects=True, vmem_limit_bytes=60 * 1024 * 1024
         ),
@@ -438,15 +488,9 @@
             transcendentals=seq_rows * units,
         ),
     )(
-        by_piece,
-        merge_gain[None],
-        merge_bias[None],
-        lax.dynamic_slice_in_dim(up_bias, tp * units, units, 0)[None],
-        lax.dynamic_slice_in_dim(down_bias, group * cols, cols, 0)[None],
-        lax.dynamic_slice_in_dim(norm_gain, tp * feats, feats, 0)[:, None],
-        kv_bias[None],
-        picks,
-        present,
+        patches[0, 0],
+        params,
+        dest,
         up_weight,
         down_weight,
         kv_weight,

time: 136 us -> 123 us (0.904)
  Pallas kernels: 119 us -> 111 us
  local copies, waits for them, and re-layouts: 13.7 us -> 8.97 us
    pallas_call x1, Pallas kernels: 119 us -> 111 us  [per_device(): pl.pallas_call(functools.partial(kernel, (n_enc, n_tp)), out_shape=(jax.S...]
    broadcast_in_dim x4 -> x1, local copies, waits for them, and re-layouts: 4.51 us -> 0.64 us  [per_device(): jnp.concatenate([merge_gain, merge_bias, kv_bias, lax.dynamic_slice_in_di...]
    unnamed x4 -> x9, local copies, waits for them, and re-layouts: 3.95 us -> 7.45 us
    dynamic_slice x3 -> x0, local copies, waits for them, and re-layouts: 2.76 us -> none  [the longest x1 1.28 us: per_device(): lax.dynamic_slice_in_dim(down_bias, group * cols, cols, 0)[None]]
    another operation x2 -> x0, local copies, waits for them, and re-layouts: 1.64 us -> none  [per_device(): patches[0, 0].reshape(own, 4, patches.shape[3]).transpose(1, 0, 2)]
where the time goes in v3:
time: 123 us
  Pallas kernels  111 us (90%)
  local copies, waits for them, and re-layouts  8.97 us (7%)
  other arithmetic  1.91 us (2%)
    pallas_call x1, Pallas kernels, per_device(): pl.pallas_call(functools.partial(kernel, (n_enc, n_tp)), out_shape=(jax.S...  111 us
    unnamed x9, local copies, waits for them, and re-layouts  7.45 us

profile of v3, /device:TPU:0, one launch (start us, length us, event | category | flops | bytes accessed | tf_op | source)
XLA Modules:
  0.0 122.9 jit_solution(5649574637393036460)
XLA Ops:
  0.6 0.7 and_select_fusion
  1.3 0.1 iota_compare_fusion
  1.4 0.1 lt.39
  1.5 1.2 fusion.dest
  2.6 0.7 constant_dynamic-update-slice_fusion.3
  3.3 0.7 constant_dynamic-update-slice_fusion.2
  4.0 0.7 constant_dynamic-update-slice_fusion.1
  4.8 0.7 dynamic-slice_dynamic-update-slice_fusion.1
  5.5 0.7 constant_dynamic-update-slice_fusion
  6.1 0.8 dynamic-slice_dynamic-update-slice_fusion
  6.9 0.6 broadcast_in_dim.16.params
  7.6 111.4 %shard_map.140 = (bf16[128,8192]{1,0:T(8,128)(2,1)}, bf16[128,2048]{1,0:T(8,128)(2,1)}) custom-call(bf16[64,1280]{1,0:T(8,128)(2,1)} %bitcast.19, f32[1,8960]{1,0:T(1,128)} %broadcast_in_dim.16.params, s32[1,64]{1,0:T(1,128)} %fusion.dest, bf16[640,1280]{1,0:T(8,128)(2,1)} %up_hbm.1, bf16[1280,1024]{1,0:T(8,128)(2,1)} %down_hbm.1, ...), custom_call_target="tpu_custom_call" | custom-call | flops 6476005376 | bytes 16842752 | tf_op jit(solution)/shard_map/pallas_call | solution.py:446
  119.0 0.0 copy-start
  119.0 3.2 %copy.23 = bf16[1,1,128,8192]{3,2,1,0:T(8,128)(2,1)} copy(bf16[1,1,128,8192]{3,2,1,0:T(8,128)(2,1)} %bitcast.16) | data formatting | bytes 4194304
  122.1 0.0 copy-done
  122.1 0.8 copy.24
  (1 shorter events, 0.0 us)
Async XLA Ops:
  119.0 3.2 %copy-start = (bf16[128,2048]{1,0:T(8,128)(2,1)S(1)}, bf16[128,2048]{1,0:T(8,128)(2,1)}, u32[]{:S(2)}) copy-start(bf16[128,2048]{1,0:T(8,128)(2,1)} %get-tuple-element.5) | copy-start | bytes 1572868

commit v4 on v3

--- a/solution.py
+++ b/solution.py
@@ -152,11 +152,58 @@
     present[...] = jnp.sum(chosen, axis=-1, keepdims=True)
     pl.semaphore_wait(barrier, groups - 1 + n_tp - 1)
 
+    quarter, half = tokens // 4, tokens // 2
+    copies_t, copies_u = [], []
+
+    def text_columns(q, of, to, where):
+        at = pl.ds(q * quarter, quarter)
+        return remote(
+            text_hbm.at[at, pl.ds(pl.multiple_of(to * feats, feats), feats)],
+            text_cols.at[of, at],
+            send_t.at[q, to],
+            recv_t.at[q, of],
+            where,
+        )
+
+    def send_columns(q):
+        for to, where in other_tps():
+            copy = text_columns(q, tp, to, where)
+            copy.start()
+            copies_t.append(copy)
+
+    def text_piece(h, src, dst, to, where):
+        at = pl.ds(h * half, half)
+        return remote(
+            text_part.at[src, at], text_in.at[dst, at], send_u.at[h, to], recv_u.at[h, dst], where
+        )
+
+    def text_half(h):
+        for q in (2 * h, 2 * h + 1):
+            for at, where in other_tps():
+                text_columns(q, at, at, where).wait_recv()
+        span = slice(h * half, (h + 1) * half)
+        for at in range(n_tp):
+            text_cols[at, span] = (text_cols[at, span].astype(F32) * norm_gain[...]).astype(BF16)
+        tile = tiles(kv_cols, 256)
+
+        @pl.loop(0, kv_cols // tile)
+        def _(i):
+            at = pl.ds(pl.multiple_of(i * tile, tile), tile)
+            lhs = text_cols[:, span].reshape(n_tp * half, feats)
+            out = jnp.dot(lhs, kv_w[:, at], preferred_element_type=F32)
+            text_part[:, span, at] = out.astype(BF16).reshape(n_tp, half, tile)
+
+        for to, where in other_tps():
+            copy = text_piece(h, to, tp, to, where)
+            copy.start()
+            copies_u.append(copy)
+
     copies_a = []
     for to, where in other_groups():
         copy = remote(split.at[to], rows.at[enc, mb, tp], send_a.at[to], recv_a.at[me], where)
         copy.start()
         copies_a.append(copy)
+    send_columns(0)
     rows[enc, mb, tp] = split[me]
     for at, where in other_groups():
         remote(split.at[at], rows.at[lax.div(at, 2), lax.rem(at, 2), tp], send_a.at[at], recv_a.at[at], where).wait_recv()
@@ -169,18 +216,6 @@
     local[0].wait()
     for at, where in other_tps():
         remote(rows.at[:, :, at], rows.at[:, :, at], send_b.at[at], recv_b.at[at], where).wait_recv()
-
-    copies_t = []
-    for to, where in other_tps():
-        copy = remote(
-            text_hbm.at[:, pl.ds(pl.multiple_of(to * feats, feats), feats)],
-            text_cols.at[tp],
-            send_t.at[to],
-            recv_t.at[tp],
-            where,
-        )
-        copy.start()
-        copies_t.append(copy)
 
     tile = tiles(units, 256)
 
@@ -192,6 +227,7 @@
             out = jnp.dot(lhs, up_w[:, at], preferred_element_type=F32)
             part[:, half, :, at] = out.astype(BF16).reshape(n_enc, seq_rows, tile)
 
+    send_columns(1)
     raise_half(1 - mb)
     to_pair = remote(part.at[:, 1 - mb], pair, send_pair, recv_pair, mate)
     to_pair.start()
@@ -204,8 +240,13 @@
         copy.start()
         copies_c.append(copy)
 
+    send_columns(2)
+    send_columns(3)
+    local[2].wait()
     local[3].wait()
     text_cols[tp] = text[:, pl.ds(pl.multiple_of(tp * feats, feats), feats)]
+
+    text_half(0)
 
     total = part[enc, mb].astype(F32) + pair[enc].astype(F32) + up_bias[...]
     for at, where in other_encs():
@@ -222,38 +263,7 @@
         copy.start()
         copies_d.append(copy)
 
-    for at, where in other_tps():
-        remote(text_cols.at[at], text_cols.at[at], send_t.at[at], recv_t.at[at], where).wait_recv()
-    local[2].wait()
-    for at in range(n_tp):
-        text_cols[at] = (text_cols[at].astype(F32) * norm_gain[...]).astype(BF16)
-    tile = tiles(kv_cols, 256)
-
-    @pl.loop(0, kv_cols // tile)
-    def _(i):
-        at = pl.ds(pl.multiple_of(i * tile, tile), tile)
-        lhs = text_cols[...].reshape(n_tp * tokens, feats)
-        out = jnp.dot(lhs, kv_w[:, at], preferred_element_type=F32)
-        text_part[:, :, at] = out.astype(BF16).reshape(n_tp, tokens, tile)
-
-    half = kv_cols // 2
-
-    def text_piece(h, src, dst, to, where):
-        at = pl.ds(h * half, half)
-        return remote(
-            text_part.at[src, :, at], text_in.at[dst, :, at], send_u.at[h, to], recv_u.at[h, dst], where
-        )
-
-    copies_u = []
-
-    def send_text(h):
-        for to, where in other_tps():
-            copy = text_piece(h, to, tp, to, where)
-            copy.start()
-            copies_u.append(copy)
-
-    send_text(0)
-
+    text_half(1)
     for at, where in other_encs():
         remote(hidden.at[at, mb], hidden.at[at, mb], send_d.at[at], recv_d.at[at], where).wait_recv()
         copy = remote(hidden.at[at, mb], hidden.at[at, mb], send_fw.at[at], recv_fw.at[at], mate)
@@ -265,41 +275,48 @@
         ).wait_recv()
 
     local[1].wait()
-    tile = tiles(cols, 256)
-
-    @pl.loop(0, cols // tile)
-    def _(i):
-        at = pl.ds(pl.multiple_of(i * tile, tile), tile)
+    wide = cols // 2
+    copies_e, copies_f = [], []
+
+    def sums_piece(h, to, dst, where):
+        at = pl.ds(h * wide, wide)
+        return remote(
+            lowered.at[:, to, :, at], low_in.at[dst, :, :, at], send_e.at[h, to], recv_e.at[h, dst], where
+        )
+
+    for h in range(2):
+        at = pl.ds(h * wide, wide)
         lhs = hidden[...].reshape(groups * seq_rows, units)
         out = jnp.dot(lhs, down_w[:, at], preferred_element_type=F32)
-        lowered[:, :, :, at] = out.astype(BF16).reshape(groups, n_tp, own, tile)
-
-    copies_e = []
-    for to, where in other_tps():
-        copy = remote(lowered.at[:, to], low_in.at[tp], send_e.at[to], recv_e.at[tp], where)
-        copy.start()
-        copies_e.append(copy)
-    for at, where in other_tps():
-        remote(lowered.at[:, at], low_in.at[at], send_e.at[at], recv_e.at[at], where).wait_recv()
-    send_text(1)
+        lowered[:, :, :, at] = out.astype(BF16).reshape(groups, n_tp, own, wide)
+        for to, where in other_tps():
+            copy = sums_piece(h, to, tp, where)
+            copy.start()
+            copies_e.append(copy)
     low_in[tp] = lowered[:, tp]
-    copies_f = []
-
-    def finish(to):
-        out = down_bias[...] + jnp.zeros((own, cols), F32)
-        for t in range(n_tp):
-            out = out + low_in[t, to].astype(F32)
-        vis_part[to] = out.astype(BF16)
-
-    for to, where in other_groups():
-        finish(to)
-        copy = remote(vis_part.at[to], visual.at[tp, me], send_f.at[to], recv_f.at[me], where)
-        copy.start()
-        copies_f.append(copy)
-    finish(me)
+
+    def rows_piece(h, to, of, where):
+        at = pl.ds(h * wide, wide)
+        return remote(
+            vis_part.at[to, :, at], visual.at[tp, of, :, at], send_f.at[h, to], recv_f.at[h, of], where
+        )
+
+    for h in range(2):
+        at = pl.ds(h * wide, wide)
+        for of, where in other_tps():
+            sums_piece(h, of, of, where).wait_recv()
+        out = low_in[0, :, :, at].astype(F32)
+        for t in range(1, n_tp):
+            out = out + low_in[t, :, :, at].astype(F32)
+        vis_part[:, :, at] = (out + down_bias[:, at]).astype(BF16)
+        for to, where in other_groups():
+            copy = rows_piece(h, to, me, where)
+            copy.start()
+            copies_f.append(copy)
     visual[tp, me] = vis_part[me]
-    for at, where in other_groups():
-        remote(vis_part.at[at], visual.at[tp, at], send_f.at[at], recv_f.at[at], where).wait_recv()
+    for h in range(2):
+        for of, where in other_groups():
+            rows_piece(h, of, of, where).wait_recv()
 
     def visual_piece(of, block, to, where):
         at = visual.at[of, pl.ds(block * per_feat, per_feat)]
@@ -478,7 +495,8 @@
             dma((4,)),
         ]
         + by_group + by_tp + [dma, dma] + by_enc + by_enc + by_enc
-        + by_tp + by_group + [dma((n_tp, n_tp))] * 2 + by_tp + by_tp + by_tp + [dma((2, n_tp))] * 2,
+        + [dma((2, n_tp))] * 2 + [dma((2, groups))] * 2 + [dma((n_tp, n_tp))] * 2 + by_tp + by_tp
+        + [dma((4, n_tp))] * 2 + [dma((2, n_tp))] * 2,
         compiler_params=pltpu.CompilerParams(
             collective_id=0, has_side_effects=True, vmem_limit_bytes=60 * 1024 * 1024
         ),

time: 123 us -> 116 us (0.943)
  Pallas kernels: 111 us -> 104 us
    pallas_call x1, Pallas kernels: 111 us -> 104 us  [per_device(): pl.pallas_call(functools.partial(kernel, (n_enc, n_tp)), out_shape=(jax.S...]
where the time goes in v4:
time: 116 us
  Pallas kernels  104 us (90%)
  local copies, waits for them, and re-layouts  8.97 us (8%)
  other arithmetic  1.91 us (2%)
    pallas_call x1, Pallas kernels, per_device(): pl.pallas_call(functools.partial(kernel, (n_enc, n_tp)), out_shape=(jax.S...  104 us
    unnamed x9, local copies, waits for them, and re-layouts  7.45 us

profile of v4, /device:TPU:0, one launch (start us, length us, event | category | flops | bytes accessed | tf_op | source)
XLA Modules:
  0.0 115.7 jit_solution(10328860927197638912)
XLA Ops:
  0.6 0.7 and_select_fusion
  1.3 0.1 iota_compare_fusion
  1.4 0.1 lt.39
  1.5 1.2 %fusion.dest = s32[1,64]{1,0:T(1,128)} fusion(pred[1,64]{1,0:T(4,128)(4,1)S(1)} %lt.39, s32[1,1,64]{2,1,0:T(1,128)} %param.15, s32[]{:T(128)S(6)} %mul.19), kind=kLoop, calls=%fused_computation.12 | loop fusion | flops 128 | bytes 580 | tf_op jit(solution)/shard_map/sub | solution.py:447
  2.6 0.7 constant_dynamic-update-slice_fusion.3
  3.3 0.7 constant_dynamic-update-slice_fusion.2
  4.0 0.7 constant_dynamic-update-slice_fusion.1
  4.8 0.7 dynamic-slice_dynamic-update-slice_fusion.1
  5.5 0.7 constant_dynamic-update-slice_fusion
  6.1 0.8 dynamic-slice_dynamic-update-slice_fusion
  6.9 0.6 broadcast_in_dim.16.params
  7.6 104.2 %shard_map.140 = (bf16[128,8192]{1,0:T(8,128)(2,1)}, bf16[128,2048]{1,0:T(8,128)(2,1)}) custom-call(bf16[64,1280]{1,0:T(8,128)(2,1)} %bitcast.19, f32[1,8960]{1,0:T(1,128)} %broadcast_in_dim.16.params, s32[1,64]{1,0:T(1,128)} %fusion.dest, bf16[640,1280]{1,0:T(8,128)(2,1)} %up_hbm.1, bf16[1280,1024]{1,0:T(8,128)(2,1)} %down_hbm.1, ...), custom_call_target="tpu_custom_call" | custom-call | flops 6476005376 | bytes 16842752 | tf_op jit(solution)/shard_map/pallas_call | solution.py:463
  111.7 0.0 copy-start
  111.7 3.2 %copy.23 = bf16[1,1,128,8192]{3,2,1,0:T(8,128)(2,1)} copy(bf16[1,1,128,8192]{3,2,1,0:T(8,128)(2,1)} %bitcast.16) | data formatting | bytes 4194304
  114.9 0.0 copy-done
  114.9 0.8 copy.24
  (1 shorter events, 0.0 us)
Async XLA Ops:
  111.7 3.2 %copy-start = (bf16[128,2048]{1,0:T(8,128)(2,1)S(1)}, bf16[128,2048]{1,0:T(8,128)(2,1)}, u32[]{:S(2)}) copy-start(bf16[128,2048]{1,0:T(8,128)(2,1)} %get-tuple-element.5) | copy-start | bytes 1572868

commit v5 on v4

--- a/solution.py
+++ b/solution.py
@@ -20,7 +20,12 @@
 def kernel(
     dims,
     patches,
-    params,
+    gain_in,
+    bias_in,
+    kv_bias_in,
+    norm_gain_in,
+    down_bias_in,
+    up_bias_in,
     dest,
     up_hbm,
     down_hbm,
@@ -51,6 +56,7 @@
     text_in,
     picks,
     present,
+    params,
     local_sem,
     send_a,
     recv_a,
@@ -135,6 +141,18 @@
     for _, to in other_tps():
         pl.semaphore_signal(barrier, inc=1, device_id=to, device_id_type=MESH)
 
+    def own_part(ref, index, size):
+        if ref.shape[0] == size:
+            return ref[...]
+        return ref[pl.ds(pl.multiple_of(index * size, size), size)]
+
+    merge_gain[...] = gain_in[...][None]
+    merge_bias[...] = bias_in[...][None]
+    kv_bias[...] = kv_bias_in[...][None]
+    norm_gain[...] = own_part(norm_gain_in, tp, feats)[None]
+    down_bias[...] = own_part(down_bias_in, me, cols)[None]
+    up_bias[...] = own_part(up_bias_in, tp, units)[None]
+
     values = patches[...].astype(F32)
     center = values - jnp.mean(values, axis=-1, keepdims=True)
     spread = jnp.mean(center * center, axis=-1, keepdims=True)
@@ -332,36 +350,50 @@
         def _(step):
             visual_piece(tp, lax.rem(to + step, n_tp), to, where).start()
 
-    tile = tiles(kv_cols, 512)
-
-    @pl.loop(0, kv_cols // tile)
-    def _(i):
-        at = pl.ds(pl.multiple_of(i * tile, tile), tile)
-        out = jnp.zeros((seq_rows, tile), F32)
-        for j in range(per_feat):
-            gain = norm_gain[:, j * cols : (j + 1) * cols]
-            lhs = visual[:, tp * per_feat + j].reshape(seq_rows, cols)
-            lhs = (lhs.astype(F32) * gain).astype(BF16)
-            out = out + jnp.dot(lhs, kv_w[j * cols : (j + 1) * cols, at], preferred_element_type=F32)
-        vkv[:, :, at] = out.astype(BF16).reshape(n_tp, own, tile)
-
-    copies_h = []
-    for to, where in other_tps():
-        copy = remote(vkv.at[to], vkv_in.at[tp], send_h.at[to], recv_h.at[tp], where)
-        copy.start()
-        copies_h.append(copy)
+    tile = tiles(kv_cols // 2, 512)
+    per_half = kv_cols // 2 // tile
+    copies_h, copies_i = [], []
+
+    def vkv_piece(h, to, of, where):
+        at = pl.ds(h * (kv_cols // 2), kv_cols // 2)
+        return remote(vkv.at[to, :, at], vkv_in.at[of, :, at], send_h.at[h, to], recv_h.at[h, of], where)
+
+    def total_piece(h, to, of, where):
+        at = vkv_all.at[of, :, pl.ds(h * (kv_cols // 2), kv_cols // 2)]
+        return remote(at, at, send_i.at[h, to], recv_i.at[h, of], where)
+
+    for h in range(2):
+
+        @pl.loop(h * per_half, (h + 1) * per_half)
+        def _(i):
+            at = pl.ds(pl.multiple_of(i * tile, tile), tile)
+            out = jnp.zeros((seq_rows, tile), F32)
+            for j in range(per_feat):
+                gain = norm_gain[:, j * cols : (j + 1) * cols]
+                lhs = visual[:, tp * per_feat + j].reshape(seq_rows, cols)
+                lhs = (lhs.astype(F32) * gain).astype(BF16)
+                out = out + jnp.dot(
+                    lhs, kv_w[j * cols : (j + 1) * cols, at], preferred_element_type=F32
+                )
+            vkv[:, :, at] = out.astype(BF16).reshape(n_tp, own, tile)
+
+        for to, where in other_tps():
+            copy = vkv_piece(h, to, tp, where)
+            copy.start()
+            copies_h.append(copy)
     vkv_in[tp] = vkv[tp]
-    for at, where in other_tps():
-        remote(vkv.at[at], vkv_in.at[at], send_h.at[at], recv_h.at[at], where).wait_recv()
-    out = vkv_in[0].astype(F32)
-    for t in range(1, n_tp):
-        out = out + vkv_in[t].astype(F32)
-    vkv_all[tp] = out.astype(BF16)
-    copies_i = []
-    for to, where in other_tps():
-        copy = remote(vkv_all.at[tp], vkv_all.at[tp], send_i.at[to], recv_i.at[tp], where)
-        copy.start()
-        copies_i.append(copy)
+    for h in range(2):
+        at = pl.ds(h * (kv_cols // 2), kv_cols // 2)
+        for of, where in other_tps():
+            vkv_piece(h, of, of, where).wait_recv()
+        out = vkv_in[0, :, at].astype(F32)
+        for t in range(1, n_tp):
+            out = out + vkv_in[t, :, at].astype(F32)
+        vkv_all[tp, :, at] = out.astype(BF16)
+        for to, where in other_tps():
+            copy = total_piece(h, to, tp, where)
+            copy.start()
+            copies_i.append(copy)
 
     for at, where in other_tps():
 
@@ -387,7 +419,8 @@
         for h in range(2):
             text_piece(h, at, at, at, where).wait_recv()
     for at, where in other_tps():
-        remote(vkv_all.at[at], vkv_all.at[at], send_i.at[at], recv_i.at[at], where).wait_recv()
+        for h in range(2):
+            total_piece(h, at, at, where).wait_recv()
 
     @pl.loop(0, kv_cols // tile)
     def _(i):
@@ -445,16 +478,9 @@
     live_rows = patch_counts[0, 0] // 4
     live = (jnp.arange(SLOT, dtype=jnp.int32)[None, :] < live_rows[:, None]).reshape(-1)
     dest = (jnp.where(live, dest_pos[0, 0], -1) - tp * tokens)[None]
-    params = jnp.concatenate(
-        [
-            merge_gain,
-            merge_bias,
-            kv_bias,
-            lax.dynamic_slice_in_dim(norm_gain, tp * feats, feats, 0),
-            lax.dynamic_slice_in_dim(down_bias, group * cols, cols, 0),
-            lax.dynamic_slice_in_dim(up_bias, tp * units, units, 0),
-        ]
-    )[None]
+    up_own = up_bias
+    if units % 128:
+        up_own = lax.dynamic_slice_in_dim(up_bias, tp * units, units, 0)
 
     dma = pltpu.SemaphoreType.DMA
     vmem = pl.BlockSpec(memory_space=pltpu.VMEM)
@@ -466,7 +492,7 @@
             jax.ShapeDtypeStruct((tokens, width), BF16),
             jax.ShapeDtypeStruct((tokens, kv_cols), BF16),
         ),
-        in_specs=[vmem] * 3 + [hbm] * 4,
+        in_specs=[vmem] * 8 + [hbm] * 4,
         out_specs=(vmem, vmem),
         scratch_shapes=[
             pltpu.VMEM((kw, units), BF16),
@@ -492,10 +518,11 @@
             pltpu.VMEM((n_tp, tokens, kv_cols), BF16),
             pltpu.VMEM((tokens, seq_rows), BF16),
             pltpu.VMEM((tokens, 1), F32),
+            pltpu.VMEM((1, 2 * patches.shape[3] + kv_cols + feats + cols + units), F32),
             dma((4,)),
         ]
         + by_group + by_tp + [dma, dma] + by_enc + by_enc + by_enc
-        + [dma((2, n_tp))] * 2 + [dma((2, groups))] * 2 + [dma((n_tp, n_tp))] * 2 + by_tp + by_tp
+        + [dma((2, n_tp))] * 2 + [dma((2, groups))] * 2 + [dma((n_tp, n_tp))] * 2 + [dma((2, n_tp))] * 4
         + [dma((4, n_tp))] * 2 + [dma((2, n_tp))] * 2,
         compiler_params=pltpu.CompilerParams(
             collective_id=0, has_side_effects=True, vmem_limit_bytes=60 * 1024 * 1024
@@ -507,7 +534,12 @@
         ),
     )(
         patches[0, 0],
-        params,
+        merge_gain,
+        merge_bias,
+        kv_bias,
+        norm_gain,
+        down_bias,
+        up_own,
         dest,
         up_weight,
         down_weight,

time: 116 us -> 111 us (0.957)
  local copies, waits for them, and re-layouts: 8.97 us -> 4.04 us
    unnamed x9 -> x4, local copies, waits for them, and re-layouts: 7.45 us -> 3.95 us
where the time goes in v5:
time: 111 us
  Pallas kernels  104 us (94%)
  local copies, waits for them, and re-layouts  4.04 us (4%)
  other arithmetic  1.91 us (2%)
    pallas_call x1, Pallas kernels, per_device(): pl.pallas_call(functools.partial(kernel, (n_enc, n_tp)), out_shape=(jax.S...  104 us
    unnamed x4, local copies, waits for them, and re-layouts  3.95 us

profile of v5, /device:TPU:0, one launch (start us, length us, event | category | flops | bytes accessed | tf_op | source)
XLA Modules:
  0.0 110.6 jit_solution(8148692357885812652)
XLA Ops:
  0.6 0.7 and_select_fusion
  1.3 0.1 iota_compare_fusion
  1.4 0.1 lt.27
  1.5 1.2 %fusion.dest = s32[1,64]{1,0:T(1,128)} fusion(pred[1,64]{1,0:T(4,128)(4,1)S(1)} %lt.27, s32[1,1,64]{2,1,0:T(1,128)} %param.15, s32[]{:T(128)S(6)} %mul.3), kind=kLoop, calls=%fused_computation.6 | loop fusion | flops 128 | bytes 580 | tf_op jit(solution)/shard_map/sub | solution.py:480
  2.6 104.0 %shard_map.140 = (bf16[128,8192]{1,0:T(8,128)(2,1)}, bf16[128,2048]{1,0:T(8,128)(2,1)}) custom-call(bf16[64,1280]{1,0:T(8,128)(2,1)} %bitcast.19, f32[1280]{0:T(1024)} %gain_in.1, f32[1280]{0:T(1024)} %bias_in.1, f32[2048]{0:T(1024)} %kv_bias_in.1, f32[8192]{0:T(1024)} %norm_gain_in.1, f32[8192]{0:T(1024)} %down_bias_in.1, f32[5120]{0:T(1024)} %up_bias_in.1, ...), custom_call_target="tpu_custom_call" | custom-call | flops 6476005376 | bytes 16842752 | tf_op jit(solution)/shard_map/pallas_call | solution.py:489
  106.7 0.0 copy-start
  106.7 3.2 %copy.17 = bf16[1,1,128,8192]{3,2,1,0:T(8,128)(2,1)} copy(bf16[1,1,128,8192]{3,2,1,0:T(8,128)(2,1)} %bitcast.16) | data formatting | bytes 4194304
  109.8 0.0 copy-done
  109.8 0.8 copy.18
Async XLA Ops:
  106.7 3.2 %copy-start = (bf16[128,2048]{1,0:T(8,128)(2,1)S(1)}, bf16[128,2048]{1,0:T(8,128)(2,1)}, u32[]{:S(2)}) copy-start(bf16[128,2048]{1,0:T(8,128)(2,1)} %get-tuple-element.5) | copy-start | bytes 1572868

commit v6 on v5

--- a/solution.py
+++ b/solution.py
@@ -235,28 +235,36 @@
     for at, where in other_tps():
         remote(rows.at[:, :, at], rows.at[:, :, at], send_b.at[at], recv_b.at[at], where).wait_recv()
 
-    tile = tiles(units, 256)
-
-    def raise_half(half):
-        @pl.loop(0, units // tile)
-        def _(i):
-            at = pl.ds(pl.multiple_of(i * tile, tile), tile)
-            lhs = rows[:, half].reshape(n_enc * seq_rows, kw)
+    send_columns(1)
+    n_cut = 2 if units % 256 == 0 else 1
+    unit_cuts = [pl.ds(u * (units // n_cut), units // n_cut) for u in range(n_cut)]
+    pair_copies = []
+    for u, at in enumerate(unit_cuts):
+        for half_at in (1 - mb, mb):
+            lhs = rows[:, half_at].reshape(n_enc * seq_rows, kw)
             out = jnp.dot(lhs, up_w[:, at], preferred_element_type=F32)
-            part[:, half, :, at] = out.astype(BF16).reshape(n_enc, seq_rows, tile)
-
-    send_columns(1)
-    raise_half(1 - mb)
-    to_pair = remote(part.at[:, 1 - mb], pair, send_pair, recv_pair, mate)
-    to_pair.start()
-    raise_half(mb)
-    to_pair.wait_recv()
+            part[:, half_at, :, at] = out.astype(BF16).reshape(n_enc, seq_rows, units // n_cut)
+            if len(pair_copies) == u:
+                copy = remote(
+                    part.at[:, 1 - mb, :, at], pair.at[:, :, at], send_pair.at[u], recv_pair.at[u], mate
+                )
+                copy.start()
+                pair_copies.append(copy)
+
+    def sum_piece(u, to, of, where):
+        at = unit_cuts[u]
+        return remote(
+            chip_sum.at[to, :, at], summed.at[of, :, at], send_c.at[u, to], recv_c.at[u, of], where
+        )
+
     copies_c = []
-    for to, where in other_encs():
-        chip_sum[to] = (part[to, mb].astype(F32) + pair[to].astype(F32)).astype(BF16)
-        copy = remote(chip_sum.at[to], summed.at[enc], send_c.at[to], recv_c.at[enc], where)
-        copy.start()
-        copies_c.append(copy)
+    for u, at in enumerate(unit_cuts):
+        pair_copies[u].wait_recv()
+        for to, where in other_encs():
+            chip_sum[to, :, at] = (part[to, mb, :, at].astype(F32) + pair[to, :, at].astype(F32)).astype(BF16)
+            copy = sum_piece(u, to, enc, where)
+            copy.start()
+            copies_c.append(copy)
 
     send_columns(2)
     send_columns(3)
@@ -266,31 +274,35 @@
 
     text_half(0)
 
-    total = part[enc, mb].astype(F32) + pair[enc].astype(F32) + up_bias[...]
-    for at, where in other_encs():
-        remote(chip_sum.at[at], summed.at[at], send_c.at[at], recv_c.at[at], where).wait_recv()
-        total = total + summed[at].astype(F32)
-    hidden[enc, mb] = (0.5 * total * (1.0 + lax.erf(total * 0.7071067811865476))).astype(BF16)
+    def hidden_piece(u, of_enc, of_mb, send, recv, to, where):
+        at = hidden.at[of_enc, of_mb, :, unit_cuts[u]]
+        return remote(at, at, send.at[u, to], recv.at[u, of_enc], where)
 
     copies_d = []
-    copy = remote(hidden.at[enc, mb], hidden.at[enc, mb], send_fw.at[enc], recv_fw.at[enc], mate)
-    copy.start()
-    copies_d.append(copy)
-    for to, where in other_encs():
-        copy = remote(hidden.at[enc, mb], hidden.at[enc, mb], send_d.at[to], recv_d.at[enc], where)
+    for u, at in enumerate(unit_cuts):
+        total = part[enc, mb, :, at].astype(F32) + pair[enc, :, at].astype(F32) + up_bias[:, at]
+        for of, where in other_encs():
+            sum_piece(u, of, of, where).wait_recv()
+            total = total + summed[of, :, at].astype(F32)
+        hidden[enc, mb, :, at] = (0.5 * total * (1.0 + lax.erf(total * 0.7071067811865476))).astype(BF16)
+        for to, where in other_encs():
+            copy = hidden_piece(u, enc, mb, send_d, recv_d, to, where)
+            copy.start()
+            copies_d.append(copy)
+        copy = hidden_piece(u, enc, mb, send_fw, recv_fw, enc, mate)
         copy.start()
         copies_d.append(copy)
 
     text_half(1)
-    for at, where in other_encs():
-        remote(hidden.at[at, mb], hidden.at[at, mb], send_d.at[at], recv_d.at[at], where).wait_recv()
-        copy = remote(hidden.at[at, mb], hidden.at[at, mb], send_fw.at[at], recv_fw.at[at], mate)
-        copy.start()
-        copies_d.append(copy)
-    for at in range(n_enc):
-        remote(
-            hidden.at[at, 1 - mb], hidden.at[at, 1 - mb], send_fw.at[at], recv_fw.at[at], mate
-        ).wait_recv()
+    for u in range(n_cut):
+        for of, where in other_encs():
+            hidden_piece(u, of, mb, send_d, recv_d, of, where).wait_recv()
+            copy = hidden_piece(u, of, mb, send_fw, recv_fw, of, mate)
+            copy.start()
+            copies_d.append(copy)
+    for u in range(n_cut):
+        for of in range(n_enc):
+            hidden_piece(u, of, 1 - mb, send_fw, recv_fw, of, mate).wait_recv()
 
     local[1].wait()
     wide = cols // 2
@@ -434,9 +446,8 @@
         mask = jnp.broadcast_to(present[...], (tokens, tile)) > 0.5
         keys_values[:, at] = (jnp.where(mask, found, plain) * scale + kv_bias[:, at]).astype(BF16)
 
-    to_pair.wait_send()
     for copies in (
-        copies_a, copies_b, copies_t, copies_c, copies_d, copies_u,
+        pair_copies, copies_a, copies_b, copies_t, copies_c, copies_d, copies_u,
         copies_e, copies_f, copies_h, copies_i,
     ):
         for copy in copies:
@@ -485,7 +496,8 @@
     dma = pltpu.SemaphoreType.DMA
     vmem = pl.BlockSpec(memory_space=pltpu.VMEM)
     hbm = pl.BlockSpec(memory_space=pl.ANY)
-    by_group, by_enc, by_tp = [dma((groups,))] * 2, [dma((n_enc,))] * 2, [dma((n_tp,))] * 2
+    n_cut = 2 if units % 256 == 0 else 1
+    by_group, by_tp = [dma((groups,))] * 2, [dma((n_tp,))] * 2
     embedded, keys_values = pl.pallas_call(
         functools.partial(kernel, (n_enc, n_tp)),
         out_shape=(
@@ -521,7 +533,7 @@
             pltpu.VMEM((1, 2 * patches.shape[3] + kv_cols + feats + cols + units), F32),
             dma((4,)),
         ]
-        + by_group + by_tp + [dma, dma] + by_enc + by_enc + by_enc
+        + by_group + by_tp + [dma((n_cut,))] * 2 + [dma((n_cut, n_enc))] * 6
         + [dma((2, n_tp))] * 2 + [dma((2, groups))] * 2 + [dma((n_tp, n_tp))] * 2 + [dma((2, n_tp))] * 4
         + [dma((4, n_tp))] * 2 + [dma((2, n_tp))] * 2,
         compiler_params=pltpu.CompilerParams(

time: 111 us -> 111 us (level)
  no operation moved by 1% of the time
where the time goes in v6:
time: 111 us
  Pallas kernels  104 us (94%)
  local copies, waits for them, and re-layouts  4.04 us (4%)
  other arithmetic  1.91 us (2%)
    pallas_call x1, Pallas kernels, per_device(): pl.pallas_call(functools.partial(kernel, (n_enc, n_tp)), out_shape=(jax.S...  104 us
    unnamed x4, local copies, waits for them, and re-layouts  3.95 us

profile of v6, /device:TPU:0, one launch (start us, length us, event | category | flops | bytes accessed | tf_op | source)
XLA Modules:
  0.0 110.9 jit_solution(14081040081543423642)
XLA Ops:
  0.6 0.7 and_select_fusion
  1.3 0.1 iota_compare_fusion
  1.4 0.1 lt.27
  1.5 1.2 %fusion.dest = s32[1,64]{1,0:T(1,128)} fusion(pred[1,64]{1,0:T(4,128)(4,1)S(1)} %lt.27, s32[1,1,64]{2,1,0:T(1,128)} %param.15, s32[]{:T(128)S(6)} %mul.3), kind=kLoop, calls=%fused_computation.6 | loop fusion | flops 128 | bytes 580 | tf_op jit(solution)/shard_map/sub | solution.py:491
  2.6 104.3 %shard_map.140 = (bf16[128,8192]{1,0:T(8,128)(2,1)}, bf16[128,2048]{1,0:T(8,128)(2,1)}) custom-call(bf16[64,1280]{1,0:T(8,128)(2,1)} %bitcast.19, f32[1280]{0:T(1024)} %gain_in.1, f32[1280]{0:T(1024)} %bias_in.1, f32[2048]{0:T(1024)} %kv_bias_in.1, f32[8192]{0:T(1024)} %norm_gain_in.1, f32[8192]{0:T(1024)} %down_bias_in.1, f32[5120]{0:T(1024)} %up_bias_in.1, ...), custom_call_target="tpu_custom_call" | custom-call | flops 6476005376 | bytes 16842752 | tf_op jit(solution)/shard_map/pallas_call | solution.py:501
  106.9 0.0 copy-start
  106.9 3.2 %copy.17 = bf16[1,1,128,8192]{3,2,1,0:T(8,128)(2,1)} copy(bf16[1,1,128,8192]{3,2,1,0:T(8,128)(2,1)} %bitcast.16) | data formatting | bytes 4194304
  110.1 0.0 copy-done
  110.1 0.8 copy.18
Async XLA Ops:
  106.9 3.2 %copy-start = (bf16[128,2048]{1,0:T(8,128)(2,1)S(1)}, bf16[128,2048]{1,0:T(8,128)(2,1)}, u32[]{:S(2)}) copy-start(bf16[128,2048]{1,0:T(8,128)(2,1)} %get-tuple-element.5) | copy-start | bytes 1572868
